TPU v7x, 512 devices: a whole 4x4x16 slice. The times are simulated.
512 devices in a mesh: grp: 8 (over z_lo), gy: 8 (over y, core), gx: 8 (over x, z_hi).
Axes of the slice: x: 4, y: 4, z: 16 (z_hi: 2, z_lo: 8; z = z_hi * 8 + z_lo), core: 2. Of those that a mesh axis runs over, the one named last changes fastest.
Arguments:
- right_side: float32 [64, 256, 1024], P('grp', 'gy', 'gx'), may hold values from -60 to 60
- reaction: float32 [64, 256, 1024], P('grp', 'gy', 'gx'), may hold values from 0.25 to 4
Outputs:
- correction: float32 [64, 256, 1024], P('grp', 'gy', 'gx')
- new_residual: float32 [64, 256, 1024], P('grp', 'gy', 'gx')
All inputs are finite; a program needn't handle non-finite values.
Results may differ from a plain program's by a relative error of at most 0.000072.
Values sent between devices are 32-bit elements; how exact they have to be, the bound alone decides.
A program may use at most 64 MiB of HBM per device.

v0:
```python
import math

import jax
import jax.numpy as jnp
from jax import lax
from jax.sharding import PartitionSpec as P

stencil_weights = (1.0, 0.5, 0.25)
stencil_center = 14.0
coarse_share = 0.5
chebyshev_taus = tuple(
    (1.0 / (1.15 + 0.85 * math.cos((2 * number - 1) * math.pi / 6.0)) for number in (1, 2, 3))
)


def extended(cells, sides, width):
    for axis, dim in sides:
        count = lax.axis_size(axis)
        ends = count - 1
        head = lax.slice_in_dim(cells, 0, width, axis=dim)
        tail = lax.slice_in_dim(cells, cells.shape[dim] - width, cells.shape[dim], axis=dim)
        cells = jnp.concatenate(
            [
                lax.ppermute(tail, axis, [(i, (i + 1) % count) for i in range(ends)]),
                cells,
                lax.ppermute(head, axis, [((i + 1) % count, i) for i in range(ends)]),
            ],
            axis=dim,
        )
    return cells


def neighbour_sum(padded, shape):
    summed = jnp.zeros(shape, jnp.float32)
    for offset_z in range(3):
        for offset_y in range(3):
            for offset_x in range(3):
                distance = abs(offset_z - 1) + abs(offset_y - 1) + abs(offset_x - 1)
                if distance > 0:
                    summed = (
                        summed
                        + stencil_weights[distance - 1]
                        * padded[
                            offset_z : offset_z + shape[0],
                            offset_y : offset_y + shape[1],
                            offset_x : offset_x + shape[2],
                        ]
                    )
    return summed


def operate(values, diagonal, padder):
    return diagonal * values - neighbour_sum(padder(values), values.shape)


def smooth(source, diagonal, padder):
    iterate = chebyshev_taus[0] * source / diagonal
    for number in (1, 2):
        residue = source - operate(iterate, diagonal, padder)
        iterate = iterate + chebyshev_taus[number] * residue / diagonal
    return iterate


def restrict_mean(values):
    planes, rows_y, rows_x = values.shape
    return values.reshape(planes // 2, 2, rows_y // 2, 2, rows_x // 2, 2).mean(axis=(1, 3, 5))


def prolong_copy(values):
    planes, rows_y, rows_x = values.shape
    spread = jnp.broadcast_to(values[:, None, :, None, :, None], (planes, 2, rows_y, 2, rows_x, 2))
    return spread.reshape(planes * 2, rows_y * 2, rows_x * 2)


def fine_padder(values):
    return extended(values, (("grp", 0), ("gy", 1), ("gx", 2)), 1)


def result_padder(values):
    return extended(values, (("grp", 0), ("gy", 1), ("gx", 2)), 1)


def middle_padder(values):
    return extended(values, (("grp", 0), ("gy", 1), ("gx", 2)), 1)


def deep_padder(values):
    return extended(values, (("grp", 0), ("gy", 1), ("gx", 2)), 1)


def per_device(right_side, reaction):
    diagonal = stencil_center + reaction
    fine_part = smooth(right_side, diagonal, fine_padder)
    source_two = restrict_mean(right_side)
    coef_two = restrict_mean(reaction)
    level_two = smooth(source_two, stencil_center + coef_two, middle_padder)
    source_three = restrict_mean(source_two)
    coef_three = restrict_mean(coef_two)
    level_three = smooth(source_three, stencil_center + coef_three, deep_padder)
    level_four = smooth(
        restrict_mean(source_three), stencil_center + restrict_mean(coef_three), deep_padder
    )
    upper_sum = level_three + prolong_copy(level_four)
    coarse = prolong_copy(level_two + prolong_copy(upper_sum))
    correction = fine_part + coarse_share * coarse
    new_residual = right_side - operate(correction, diagonal, result_padder)
    return (correction, new_residual)


def solution(mesh):
    in_specs = (P("grp", "gy", "gx"), P("grp", "gy", "gx"))
    out_specs = (P("grp", "gy", "gx"), P("grp", "gy", "gx"))
    return jax.shard_map(
        per_device, mesh=mesh, in_specs=in_specs, out_specs=out_specs, check_vma=False
    )
```

profile of v0, /device:TPU:40, one launch (start us, length us, event | category | flops | bytes accessed | tf_op | source)
XLA Modules:
  0.0 420.5 jit_solution(17434343023935939042)
XLA Ops:
  0.6 10.6 %reshape.92 = f32[4,2,16,2,64,2]{5,4,3,2,1,0:T(8,128)} reshape(f32[8,32,128]{2,1,0:T(8,128)} %param.2) | data formatting | bytes 262144 | tf_op jit(solution)/shard_map/reshape | solution.py:66
  11.2 9.7 %reshape.93 = f32[4,2,16,2,64,2]{5,4,3,2,1,0:T(8,128)} reshape(f32[8,32,128]{2,1,0:T(8,128)S(1)} %copy-done.2) | data formatting | bytes 262144 | tf_op jit(solution)/shard_map/reshape | solution.py:66
  20.9 4.0 reduce_sum.68
  24.9 4.0 reduce_sum.69
  33.9 3.8 collective-permute-start.36
  39.8 3.8 collective-permute-start.24
  50.1 6.6 %collective-permute-done.38 = f32[3,1,16]{2,1,0:T(1,128)S(1)} collective-permute-done((f32[3,1,16]{2,1,0:T(1,128)S(1)}, f32[3,1,16]{2,1,0:T(1,128)S(1)}, u32[]{:S(2)}, u32[]{:S(2)}) %collective-permute-start.38) | collective-permute-done | bytes 224 | tf_op jit(solution)/shard_map/ppermute | solution.py:24
  56.8 11.5 %collective-permute-start.40 = (f32[3,6,1]{2,1,0:T(8,128)S(1)}, f32[3,6,1]{2,1,0:T(8,128)S(1)}, u32[]{:S(2)}, u32[]{:S(2)}) collective-permute-start(f32[3,6,1]{2,1,0:T(8,128)S(1)} %get-tuple-element.69), channel_id=1, source_target_pairs={{0,1},{1,2},{2,3},{3,4},{4,5},{5,6},{6,7},{8,9},{9,10},{10,11},{11... | collective-permute-start | bytes 224 | tf_op jit(solution)/shard_map/ppermute | solution.py:24
  69.7 12.9 %collective-permute-done.41 = f32[3,6,1]{2,1,0:T(8,128)S(1)} collective-permute-done((f32[3,6,1]{2,1,0:T(8,128)S(1)}, f32[3,6,1]{2,1,0:T(8,128)S(1)}, u32[]{:S(2)}, u32[]{:S(2)}) %collective-permute-start.41) | collective-permute-done | bytes 104 | tf_op jit(solution)/shard_map/ppermute | solution.py:26
  84.7 3.9 collective-permute-start.42
  88.7 3.4 collective-permute-start.12
  98.9 3.2 collective-permute-start.27
  111.5 13.1 %collective-permute-start.46 = (f32[3,6,1]{2,1,0:T(8,128)S(1)}, f32[3,6,1]{2,1,0:T(8,128)S(1)}, u32[]{:S(2)}, u32[]{:S(2)}) collective-permute-start(f32[3,6,1]{2,1,0:T(8,128)S(1)} %get-tuple-element.67), channel_id=1, source_target_pairs={{0,1},{1,2},{2,3},{3,4},{4,5},{5,6},{6,7},{8,9},{9,10},{10,11},{11... | collective-permute-start | bytes 224 | tf_op jit(solution)/shard_map/ppermute | solution.py:24
  128.3 11.5 %collective-permute-done.47 = f32[3,6,1]{2,1,0:T(8,128)S(1)} collective-permute-done((f32[3,6,1]{2,1,0:T(8,128)S(1)}, f32[3,6,1]{2,1,0:T(8,128)S(1)}, u32[]{:S(2)}, u32[]{:S(2)}) %collective-permute-start.47) | collective-permute-done | bytes 104 | tf_op jit(solution)/shard_map/ppermute | solution.py:26
  139.9 4.7 %collective-permute-start.30 = (f32[1,8,32]{2,1,0:T(8,128)S(1)}, f32[1,8,32]{2,1,0:T(8,128)S(1)}, u32[]{:S(2)}, u32[]{:S(2)}) collective-permute-start(f32[1,8,32]{2,1,0:T(8,128)S(1)} %get-tuple-element.78), channel_id=1, source_target_pairs={{0,64},{64,128},{128,192},{192,256},{256,320},{320,384},{384,448},... | collective-permute-start | bytes 3080 | tf_op jit(solution)/shard_map/ppermute | solution.py:24
  150.5 4.4 %collective-permute-start = (f32[1,32,128]{2,1,0:T(8,128)S(1)}, f32[1,32,128]{2,1,0:T(8,128)S(1)}, u32[]{:S(2)}, u32[]{:S(2)}) collective-permute-start(f32[1,32,128]{2,1,0:T(8,128)S(1)} %get-tuple-element.30), channel_id=1, source_target_pairs={{0,64},{64,128},{128,192},{192,256},{256,320},{320,384},{384,448},... | collective-permute-start | bytes 49160 | tf_op jit(solution)/shard_map/ppermute | solution.py:24
  159.8 13.5 %collective-permute-start.34 = (f32[4,10,1]{2,1,0:T(8,128)S(1)}, f32[4,10,1]{2,1,0:T(8,128)S(1)}, u32[]{:S(2)}, u32[]{:S(2)}) collective-permute-start(f32[4,10,1]{2,1,0:T(8,128)S(1)} %get-tuple-element.55), channel_id=1, source_target_pairs={{0,1},{1,2},{2,3},{3,4},{4,5},{5,6},{6,7},{8,9},{9,10},{10,11},{11... | collective-permute-start | bytes 488 | tf_op jit(solution)/shard_map/ppermute | solution.py:24
  181.2 22.4 %collective-permute-done.17 = f32[6,18,1]{2,1,0:T(8,128)S(1)} collective-permute-done((f32[6,18,1]{2,1,0:T(8,128)S(1)}, f32[6,18,1]{2,1,0:T(8,128)S(1)}, u32[]{:S(2)}, u32[]{:S(2)}) %collective-permute-start.17) | collective-permute-done | bytes 464 | tf_op jit(solution)/shard_map/ppermute | solution.py:26
  205.8 3.9 collective-permute-start.18
  218.3 6.0 %collective-permute-start.22 = (f32[6,18,1]{2,1,0:T(8,128)S(1)}, f32[6,18,1]{2,1,0:T(8,128)S(1)}, u32[]{:S(2)}, u32[]{:S(2)}) collective-permute-start(f32[6,18,1]{2,1,0:T(8,128)S(1)} %get-tuple-element.32), channel_id=1, source_target_pairs={{0,1},{1,2},{2,3},{3,4},{4,5},{5,6},{6,7},{8,9},{9,10},{10,11},{11... | collective-permute-start | bytes 1304 | tf_op jit(solution)/shard_map/ppermute | solution.py:24
  232.7 13.3 %collective-permute-start.4 = (f32[10,34,1]{2,1,0:T(8,128)S(1)}, f32[10,34,1]{2,1,0:T(8,128)S(1)}, u32[]{:S(2)}, u32[]{:S(2)}) collective-permute-start(f32[10,34,1]{2,1,0:T(8,128)S(1)} %get-tuple-element.6), channel_id=1, source_target_pairs={{0,1},{1,2},{2,3},{3,4},{4,5},{5,6},{6,7},{8,9},{9,10},{10,11},{11... | collective-permute-start | bytes 4088 | tf_op jit(solution)/shard_map/ppermute | solution.py:24
  247.3 4.5 %collective-permute-done.4 = f32[10,34,1]{2,1,0:T(8,128)S(1)} collective-permute-done((f32[10,34,1]{2,1,0:T(8,128)S(1)}, f32[10,34,1]{2,1,0:T(8,128)S(1)}, u32[]{:S(2)}, u32[]{:S(2)}) %collective-permute-start.4) | collective-permute-done | bytes 1392 | tf_op jit(solution)/shard_map/ppermute | solution.py:24
  251.8 35.6 %collective-permute-done.5 = f32[10,34,1]{2,1,0:T(8,128)S(1)} collective-permute-done((f32[10,34,1]{2,1,0:T(8,128)S(1)}, f32[10,34,1]{2,1,0:T(8,128)S(1)}, u32[]{:S(2)}, u32[]{:S(2)}) %collective-permute-start.5) | collective-permute-done | bytes 1392 | tf_op jit(solution)/shard_map/ppermute | solution.py:26
  290.0 3.9 collective-permute-start.6
  300.4 3.9 broadcast_in_dim.29
  304.3 6.9 %mul.863 = f32[8,32,128]{2,1,0:T(8,128)S(1)} reshape(f32[4,2,16,2,64,2]{5,4,3,2,1,0:T(8,128)} %broadcast_in_dim.29) | data formatting | bytes 262144 | tf_op jit(solution)/shard_map/mul | solution.py:105
  314.1 3.2 collective-permute-done.10
  317.3 39.8 %collective-permute-done.11 = f32[10,34,1]{2,1,0:T(8,128)S(1)} collective-permute-done((f32[10,34,1]{2,1,0:T(8,128)S(1)}, f32[10,34,1]{2,1,0:T(8,128)S(1)}, u32[]{:S(2)}, u32[]{:S(2)}) %collective-permute-start.11) | collective-permute-done | bytes 1392 | tf_op jit(solution)/shard_map/ppermute | solution.py:26
  359.7 3.9 collective-permute-start.48
  372.4 7.3 %collective-permute-start.52 = (f32[10,34,1]{2,1,0:T(8,128)S(1)}, f32[10,34,1]{2,1,0:T(8,128)S(1)}, u32[]{:S(2)}, u32[]{:S(2)}) collective-permute-start(f32[10,34,1]{2,1,0:T(8,128)S(1)} %get-tuple-element.2), channel_id=1, source_target_pairs={{0,1},{1,2},{2,3},{3,4},{4,5},{5,6},{6,7},{8,9},{9,10},{10,11},{11... | collective-permute-start | bytes 4088 | tf_op jit(solution)/shard_map/ppermute | solution.py:24
  381.0 9.7 %collective-permute-done.52 = f32[10,34,1]{2,1,0:T(8,128)S(1)} collective-permute-done((f32[10,34,1]{2,1,0:T(8,128)S(1)}, f32[10,34,1]{2,1,0:T(8,128)S(1)}, u32[]{:S(2)}, u32[]{:S(2)}) %collective-permute-start.52) | collective-permute-done | bytes 1392 | tf_op jit(solution)/shard_map/ppermute | solution.py:24
  390.7 28.5 %collective-permute-done.53 = f32[10,34,1]{2,1,0:T(8,128)S(1)} collective-permute-done((f32[10,34,1]{2,1,0:T(8,128)S(1)}, f32[10,34,1]{2,1,0:T(8,128)S(1)}, u32[]{:S(2)}, u32[]{:S(2)}) %collective-permute-start.53) | collective-permute-done | bytes 1392 | tf_op jit(solution)/shard_map/ppermute | solution.py:26
  (161 shorter events, 101.4 us)
Async XLA Ops:
  31.9 13.8 %collective-permute-start.37 = (f32[1,4,16]{2,1,0:T(4,128)S(1)}, f32[1,4,16]{2,1,0:T(4,128)S(1)}, u32[]{:S(2)}, u32[]{:S(2)}) collective-permute-start(f32[1,4,16]{2,1,0:T(4,128)S(1)} %bitcast_divide_fusion), channel_id=1, source_target_pairs={{64,0},{128,64},{192,128},{256,192},{320,256},{384,320},{448,384},... | collective-permute-start | bytes 776 | tf_op jit(solution)/shard_map/ppermute | solution.py:26
  33.9 11.7 %collective-permute-start.36 = (f32[1,4,16]{2,1,0:T(4,128)S(1)}, f32[1,4,16]{2,1,0:T(4,128)S(1)}, u32[]{:S(2)}, u32[]{:S(2)}) collective-permute-start(f32[1,4,16]{2,1,0:T(4,128)S(1)} %bitcast_divide_fusion), channel_id=1, source_target_pairs={{0,64},{64,128},{128,192},{192,256},{256,320},{320,384},{384,448},... | collective-permute-start | bytes 776 | tf_op jit(solution)/shard_map/ppermute | solution.py:24
  37.7 56.8 %collective-permute-start.25 = (f32[1,8,32]{2,1,0:T(8,128)S(1)}, f32[1,8,32]{2,1,0:T(8,128)S(1)}, u32[]{:S(2)}, u32[]{:S(2)}) collective-permute-start(f32[1,8,32]{2,1,0:T(8,128)S(1)} %get-tuple-element.81), channel_id=1, source_target_pairs={{64,0},{128,64},{192,128},{256,192},{320,256},{384,320},{448,384},... | collective-permute-start | bytes 3080 | tf_op jit(solution)/shard_map/ppermute | solution.py:26
  39.8 56.7 %collective-permute-start.24 = (f32[1,8,32]{2,1,0:T(8,128)S(1)}, f32[1,8,32]{2,1,0:T(8,128)S(1)}, u32[]{:S(2)}, u32[]{:S(2)}) collective-permute-start(f32[1,8,32]{2,1,0:T(8,128)S(1)} %get-tuple-element.80), channel_id=1, source_target_pairs={{0,64},{64,128},{128,192},{192,256},{256,320},{320,384},{384,448},... | collective-permute-start | bytes 3080 | tf_op jit(solution)/shard_map/ppermute | solution.py:24
  43.6 111.3 %collective-permute-start.13 = (f32[1,16,64]{2,1,0:T(8,128)S(1)}, f32[1,16,64]{2,1,0:T(8,128)S(1)}, u32[]{:S(2)}, u32[]{:S(2)}) collective-permute-start(f32[1,16,64]{2,1,0:T(8,128)S(1)} %get-tuple-element.51), channel_id=1, source_target_pairs={{64,0},{128,64},{192,128},{256,192},{320,256},{384,320},{448,384},... | collective-permute-start | bytes 12296 | tf_op jit(solution)/shard_map/ppermute | solution.py:26
  47.6 9.1 %collective-permute-start.38 = (f32[3,1,16]{2,1,0:T(1,128)S(1)}, f32[3,1,16]{2,1,0:T(1,128)S(1)}, u32[]{:S(2)}, u32[]{:S(2)}) collective-permute-start(f32[3,1,16]{2,1,0:T(1,128)S(1)} %get-tuple-element.84), channel_id=1, source_target_pairs={{0,8},{8,16},{16,24},{24,32},{32,40},{40,48},{48,56},{1,9},{9,17},... | collective-permute-start | bytes 584 | tf_op jit(solution)/shard_map/ppermute | solution.py:24
  56.8 12.9 %collective-permute-start.40 = (f32[3,6,1]{2,1,0:T(8,128)S(1)}, f32[3,6,1]{2,1,0:T(8,128)S(1)}, u32[]{:S(2)}, u32[]{:S(2)}) collective-permute-start(f32[3,6,1]{2,1,0:T(8,128)S(1)} %get-tuple-element.69), channel_id=1, source_target_pairs={{0,1},{1,2},{2,3},{3,4},{4,5},{5,6},{6,7},{8,9},{9,10},{10,11},{11... | collective-permute-start | bytes 224 | tf_op jit(solution)/shard_map/ppermute | solution.py:24
  68.3 14.3 %collective-permute-start.41 = (f32[3,6,1]{2,1,0:T(8,128)S(1)}, f32[3,6,1]{2,1,0:T(8,128)S(1)}, u32[]{:S(2)}, u32[]{:S(2)}) collective-permute-start(f32[3,6,1]{2,1,0:T(8,128)S(1)} %get-tuple-element.70), channel_id=1, source_target_pairs={{1,0},{2,1},{3,2},{4,3},{5,4},{6,5},{7,6},{9,8},{10,9},{11,10},{12... | collective-permute-start | bytes 224 | tf_op jit(solution)/shard_map/ppermute | solution.py:26
  84.7 7.3 %collective-permute-start.42 = (f32[1,4,16]{2,1,0:T(4,128)S(1)}, f32[1,4,16]{2,1,0:T(4,128)S(1)}, u32[]{:S(2)}, u32[]{:S(2)}) collective-permute-start(f32[1,4,16]{2,1,0:T(4,128)S(1)} %fusion.222), channel_id=1, source_target_pairs={{0,64},{64,128},{128,192},{192,256},{256,320},{320,384},{384,448},... | collective-permute-start | bytes 776 | tf_op jit(solution)/shard_map/ppermute | solution.py:24
  88.7 66.2 %collective-permute-start.12 = (f32[1,16,64]{2,1,0:T(8,128)S(1)}, f32[1,16,64]{2,1,0:T(8,128)S(1)}, u32[]{:S(2)}, u32[]{:S(2)}) collective-permute-start(f32[1,16,64]{2,1,0:T(8,128)S(1)} %get-tuple-element.50), channel_id=1, source_target_pairs={{0,64},{64,128},{128,192},{192,256},{256,320},{320,384},{384,448},... | collective-permute-start | bytes 12296 | tf_op jit(solution)/shard_map/ppermute | solution.py:24
  92.1 133.5 %collective-permute-start.1 = (f32[1,32,128]{2,1,0:T(8,128)S(1)}, f32[1,32,128]{2,1,0:T(8,128)S(1)}, u32[]{:S(2)}, u32[]{:S(2)}) collective-permute-start(f32[1,32,128]{2,1,0:T(8,128)S(1)} %get-tuple-element.31), channel_id=1, source_target_pairs={{64,0},{128,64},{192,128},{256,192},{320,256},{384,320},{448,384},... | collective-permute-start | bytes 49160 | tf_op jit(solution)/shard_map/ppermute | solution.py:26
  110.0 14.9 %collective-permute-start.29 = (f32[4,10,1]{2,1,0:T(8,128)S(1)}, f32[4,10,1]{2,1,0:T(8,128)S(1)}, u32[]{:S(2)}, u32[]{:S(2)}) collective-permute-start(f32[4,10,1]{2,1,0:T(8,128)S(1)} %get-tuple-element.58), channel_id=1, source_target_pairs={{1,0},{2,1},{3,2},{4,3},{5,4},{6,5},{7,6},{9,8},{10,9},{11,10},{12... | collective-permute-start | bytes 488 | tf_op jit(solution)/shard_map/ppermute | solution.py:26
  111.5 14.9 %collective-permute-start.46 = (f32[3,6,1]{2,1,0:T(8,128)S(1)}, f32[3,6,1]{2,1,0:T(8,128)S(1)}, u32[]{:S(2)}, u32[]{:S(2)}) collective-permute-start(f32[3,6,1]{2,1,0:T(8,128)S(1)} %get-tuple-element.67), channel_id=1, source_target_pairs={{0,1},{1,2},{2,3},{3,4},{4,5},{5,6},{6,7},{8,9},{9,10},{10,11},{11... | collective-permute-start | bytes 224 | tf_op jit(solution)/shard_map/ppermute | solution.py:24
  124.9 15.0 %collective-permute-start.47 = (f32[3,6,1]{2,1,0:T(8,128)S(1)}, f32[3,6,1]{2,1,0:T(8,128)S(1)}, u32[]{:S(2)}, u32[]{:S(2)}) collective-permute-start(f32[3,6,1]{2,1,0:T(8,128)S(1)} %get-tuple-element.68), channel_id=1, source_target_pairs={{1,0},{2,1},{3,2},{4,3},{5,4},{6,5},{7,6},{9,8},{10,9},{11,10},{12... | collective-permute-start | bytes 224 | tf_op jit(solution)/shard_map/ppermute | solution.py:26
  126.4 18.2 %collective-permute-start.31 = (f32[1,8,32]{2,1,0:T(8,128)S(1)}, f32[1,8,32]{2,1,0:T(8,128)S(1)}, u32[]{:S(2)}, u32[]{:S(2)}) collective-permute-start(f32[1,8,32]{2,1,0:T(8,128)S(1)} %get-tuple-element.79), channel_id=1, source_target_pairs={{64,0},{128,64},{192,128},{256,192},{320,256},{384,320},{448,384},... | collective-permute-start | bytes 3080 | tf_op jit(solution)/shard_map/ppermute | solution.py:26
  147.8 7.1 %collective-permute-start.32 = (f32[4,1,32]{2,1,0:T(1,128)S(1)}, f32[4,1,32]{2,1,0:T(1,128)S(1)}, u32[]{:S(2)}, u32[]{:S(2)}) collective-permute-start(f32[4,1,32]{2,1,0:T(1,128)S(1)} %get-tuple-element.63), channel_id=1, source_target_pairs={{0,8},{8,16},{16,24},{24,32},{32,40},{40,48},{48,56},{1,9},{9,17},... | collective-permute-start | bytes 1544 | tf_op jit(solution)/shard_map/ppermute | solution.py:24
  150.5 75.1 %collective-permute-start = (f32[1,32,128]{2,1,0:T(8,128)S(1)}, f32[1,32,128]{2,1,0:T(8,128)S(1)}, u32[]{:S(2)}, u32[]{:S(2)}) collective-permute-start(f32[1,32,128]{2,1,0:T(8,128)S(1)} %get-tuple-element.30), channel_id=1, source_target_pairs={{0,64},{64,128},{128,192},{192,256},{256,320},{320,384},{384,448},... | collective-permute-start | bytes 49160 | tf_op jit(solution)/shard_map/ppermute | solution.py:24
  154.9 18.4 %collective-permute-start.15 = (f32[6,1,64]{2,1,0:T(1,128)S(1)}, f32[6,1,64]{2,1,0:T(1,128)S(1)}, u32[]{:S(2)}, u32[]{:S(2)}) collective-permute-start(f32[6,1,64]{2,1,0:T(1,128)S(1)} %get-tuple-element.47), channel_id=1, source_target_pairs={{8,0},{16,8},{24,16},{32,24},{40,32},{48,40},{56,48},{9,1},{17,9},... | collective-permute-start | bytes 4616 | tf_op jit(solution)/shard_map/ppermute | solution.py:26
  157.8 15.5 %collective-permute-start.14 = (f32[6,1,64]{2,1,0:T(1,128)S(1)}, f32[6,1,64]{2,1,0:T(1,128)S(1)}, u32[]{:S(2)}, u32[]{:S(2)}) collective-permute-start(f32[6,1,64]{2,1,0:T(1,128)S(1)} %get-tuple-element.46), channel_id=1, source_target_pairs={{0,8},{8,16},{16,24},{24,32},{32,40},{40,48},{48,56},{1,9},{9,17},... | collective-permute-start | bytes 4616 | tf_op jit(solution)/shard_map/ppermute | solution.py:24
  159.8 46.0 %collective-permute-start.34 = (f32[4,10,1]{2,1,0:T(8,128)S(1)}, f32[4,10,1]{2,1,0:T(8,128)S(1)}, u32[]{:S(2)}, u32[]{:S(2)}) collective-permute-start(f32[4,10,1]{2,1,0:T(8,128)S(1)} %get-tuple-element.55), channel_id=1, source_target_pairs={{0,1},{1,2},{2,3},{3,4},{4,5},{5,6},{6,7},{8,9},{9,10},{10,11},{11... | collective-permute-start | bytes 488 | tf_op jit(solution)/shard_map/ppermute | solution.py:24
  173.5 6.4 %collective-permute-start.16 = (f32[6,18,1]{2,1,0:T(8,128)S(1)}, f32[6,18,1]{2,1,0:T(8,128)S(1)}, u32[]{:S(2)}, u32[]{:S(2)}) collective-permute-start(f32[6,18,1]{2,1,0:T(8,128)S(1)} %get-tuple-element.34), channel_id=1, source_target_pairs={{0,1},{1,2},{2,3},{3,4},{4,5},{5,6},{6,7},{8,9},{9,10},{10,11},{11... | collective-permute-start | bytes 1304 | tf_op jit(solution)/shard_map/ppermute | solution.py:24
  176.4 27.2 %collective-permute-start.17 = (f32[6,18,1]{2,1,0:T(8,128)S(1)}, f32[6,18,1]{2,1,0:T(8,128)S(1)}, u32[]{:S(2)}, u32[]{:S(2)}) collective-permute-start(f32[6,18,1]{2,1,0:T(8,128)S(1)} %get-tuple-element.35), channel_id=1, source_target_pairs={{1,0},{2,1},{3,2},{4,3},{5,4},{6,5},{7,6},{9,8},{10,9},{11,10},{12... | collective-permute-start | bytes 1304 | tf_op jit(solution)/shard_map/ppermute | solution.py:26
  179.9 29.9 %collective-permute-start.35 = (f32[4,10,1]{2,1,0:T(8,128)S(1)}, f32[4,10,1]{2,1,0:T(8,128)S(1)}, u32[]{:S(2)}, u32[]{:S(2)}) collective-permute-start(f32[4,10,1]{2,1,0:T(8,128)S(1)} %get-tuple-element.56), channel_id=1, source_target_pairs={{1,0},{2,1},{3,2},{4,3},{5,4},{6,5},{7,6},{9,8},{10,9},{11,10},{12... | collective-permute-start | bytes 488 | tf_op jit(solution)/shard_map/ppermute | solution.py:26
  218.3 75.6 %collective-permute-start.22 = (f32[6,18,1]{2,1,0:T(8,128)S(1)}, f32[6,18,1]{2,1,0:T(8,128)S(1)}, u32[]{:S(2)}, u32[]{:S(2)}) collective-permute-start(f32[6,18,1]{2,1,0:T(8,128)S(1)} %get-tuple-element.32), channel_id=1, source_target_pairs={{0,1},{1,2},{2,3},{3,4},{4,5},{5,6},{6,7},{8,9},{9,10},{10,11},{11... | collective-permute-start | bytes 1304 | tf_op jit(solution)/shard_map/ppermute | solution.py:24
  224.3 69.7 %collective-permute-start.23 = (f32[6,18,1]{2,1,0:T(8,128)S(1)}, f32[6,18,1]{2,1,0:T(8,128)S(1)}, u32[]{:S(2)}, u32[]{:S(2)}) collective-permute-start(f32[6,18,1]{2,1,0:T(8,128)S(1)} %get-tuple-element.33), channel_id=1, source_target_pairs={{1,0},{2,1},{3,2},{4,3},{5,4},{6,5},{7,6},{9,8},{10,9},{11,10},{12... | collective-permute-start | bytes 1304 | tf_op jit(solution)/shard_map/ppermute | solution.py:26
  232.7 19.2 %collective-permute-start.4 = (f32[10,34,1]{2,1,0:T(8,128)S(1)}, f32[10,34,1]{2,1,0:T(8,128)S(1)}, u32[]{:S(2)}, u32[]{:S(2)}) collective-permute-start(f32[10,34,1]{2,1,0:T(8,128)S(1)} %get-tuple-element.6), channel_id=1, source_target_pairs={{0,1},{1,2},{2,3},{3,4},{4,5},{5,6},{6,7},{8,9},{9,10},{10,11},{11... | collective-permute-start | bytes 4088 | tf_op jit(solution)/shard_map/ppermute | solution.py:24
  245.9 41.5 %collective-permute-start.5 = (f32[10,34,1]{2,1,0:T(8,128)S(1)}, f32[10,34,1]{2,1,0:T(8,128)S(1)}, u32[]{:S(2)}, u32[]{:S(2)}) collective-permute-start(f32[10,34,1]{2,1,0:T(8,128)S(1)} %get-tuple-element.7), channel_id=1, source_target_pairs={{1,0},{2,1},{3,2},{4,3},{5,4},{6,5},{7,6},{9,8},{10,9},{11,10},{12... | collective-permute-start | bytes 4088 | tf_op jit(solution)/shard_map/ppermute | solution.py:26
  295.7 15.5 %collective-permute-start.9 = (f32[10,1,128]{2,1,0:T(1,128)S(1)}, f32[10,1,128]{2,1,0:T(1,128)S(1)}, u32[]{:S(2)}, u32[]{:S(2)}) collective-permute-start(f32[10,1,128]{2,1,0:T(1,128)S(1)} %get-tuple-element.21), channel_id=1, source_target_pairs={{8,0},{16,8},{24,16},{32,24},{40,32},{48,40},{56,48},{9,1},{17,9},... | collective-permute-start | bytes 15368 | tf_op jit(solution)/shard_map/ppermute | solution.py:26
  297.6 13.6 %collective-permute-start.8 = (f32[10,1,128]{2,1,0:T(1,128)S(1)}, f32[10,1,128]{2,1,0:T(1,128)S(1)}, u32[]{:S(2)}, u32[]{:S(2)}) collective-permute-start(f32[10,1,128]{2,1,0:T(1,128)S(1)} %get-tuple-element.20), channel_id=1, source_target_pairs={{0,8},{8,16},{16,24},{24,32},{32,40},{40,48},{48,56},{1,9},{9,17},... | collective-permute-start | bytes 15368 | tf_op jit(solution)/shard_map/ppermute | solution.py:24
  312.8 44.3 %collective-permute-start.11 = (f32[10,34,1]{2,1,0:T(8,128)S(1)}, f32[10,34,1]{2,1,0:T(8,128)S(1)}, u32[]{:S(2)}, u32[]{:S(2)}) collective-permute-start(f32[10,34,1]{2,1,0:T(8,128)S(1)} %get-tuple-element.5), channel_id=1, source_target_pairs={{1,0},{2,1},{3,2},{4,3},{5,4},{6,5},{7,6},{9,8},{10,9},{11,10},{12... | collective-permute-start | bytes 4088 | tf_op jit(solution)/shard_map/ppermute | solution.py:26
  372.4 18.3 %collective-permute-start.52 = (f32[10,34,1]{2,1,0:T(8,128)S(1)}, f32[10,34,1]{2,1,0:T(8,128)S(1)}, u32[]{:S(2)}, u32[]{:S(2)}) collective-permute-start(f32[10,34,1]{2,1,0:T(8,128)S(1)} %get-tuple-element.2), channel_id=1, source_target_pairs={{0,1},{1,2},{2,3},{3,4},{4,5},{5,6},{6,7},{8,9},{9,10},{10,11},{11... | collective-permute-start | bytes 4088 | tf_op jit(solution)/shard_map/ppermute | solution.py:24
  379.7 39.5 %collective-permute-start.53 = (f32[10,34,1]{2,1,0:T(8,128)S(1)}, f32[10,34,1]{2,1,0:T(8,128)S(1)}, u32[]{:S(2)}, u32[]{:S(2)}) collective-permute-start(f32[10,34,1]{2,1,0:T(8,128)S(1)} %get-tuple-element.3), channel_id=1, source_target_pairs={{1,0},{2,1},{3,2},{4,3},{5,4},{6,5},{7,6},{9,8},{10,9},{11,10},{12... | collective-permute-start | bytes 4088 | tf_op jit(solution)/shard_map/ppermute | solution.py:26
  (25 other events, 213.1 us)
where the time goes:
time: 422 us; the launch traced here: 421 us
  waiting for transfers between devices  193 us (46%)
  starting transfers between devices  178 us (42%)
  local copies, waits for them, and re-layouts  35.2 us (8%)
  other arithmetic  13 us (3%)
    ppermute x27, waiting for transfers between devices, extended(): lax.ppermute(head, axis, [((i + 1) % count, i) for i in range(ends)])  151 us
    ppermute x27, starting transfers between devices, extended(): lax.ppermute(tail, axis, [(i, (i + 1) % count) for i in range(ends)])  128 us
    ppermute x27, starting transfers between devices, extended(): lax.ppermute(head, axis, [((i + 1) % count, i) for i in range(ends)])  49.2 us
    ppermute x27, waiting for transfers between devices, extended(): lax.ppermute(tail, axis, [(i, (i + 1) % count) for i in range(ends)])  42 us
    reshape x2, local copies, waits for them, and re-layouts, restrict_mean(): values.reshape(planes // 2, 2, rows_y // 2, 2, rows_x // 2, 2)  20.3 us
    reduce_sum x7, other arithmetic, restrict_mean(): values.reshape(planes // 2, 2, rows_y // 2, 2, rows_x // 2, 2)  8.55 us
  transfers between devices with their start and end apart: 54, of which 22 were waited for; matrix products, arithmetic and copies ran while one was open for 4% of the time, Pallas kernels for 0%

commit v1 on v0

v1 whole, which is shorter than its diff:
```python
import functools
import math

import jax
import jax.numpy as jnp
from jax import lax
from jax.experimental import pallas as pl
from jax.experimental.pallas import tpu as pltpu
from jax.sharding import PartitionSpec as P

MESH = pl.DeviceIdType.MESH
AXES = ("grp", "gy", "gx")
TAUS = tuple(1.0 / (1.15 + 0.85 * math.cos((2 * k - 1) * math.pi / 6.0)) for k in (1, 2, 3))
EXACT = lax.Precision.HIGHEST
LANES = 128
HALO = 3
DEPTH = (8, 4, 2, 1)
ROWS = (32, 16, 8, 4)
COLS = (128, 64, 32, 16)
SENT = (32, 16, 8, 8)
TALL = (48, 32, 24, 24)
LANE0 = (0, 0, 60, 84)
ROW0 = (0, 48, 48, 0)
MSG_ROWS = 80


def iota(shape, dim):
    return lax.broadcasted_iota(jnp.int32, shape, dim)


def put(cond, value, other):
    return jnp.where(cond, value, other)


def extended_plane(ext, level, a, z):
    if level < 3:
        return ext[level][a, z]
    tile = put(iota((8, LANES), 0) < 4, ext[3][a, z, 8:16], ext[3][a, z, 16:24])
    return jnp.concatenate([ext[3][a, z, 0:8], tile], axis=0)


def exchange(s_hbm, c_hbm, e1, e2, e3, e4, got, sums2, sums3, sums4, msg, in_sem, zs, zr, ys, yr, xs, xr):
    ext = (e1, e2, e3, e4)
    place = tuple(lax.axis_index(a) for a in AXES)
    count = tuple(lax.axis_size(a) for a in AXES)

    def exists(dim, step):
        if step > 0:
            return place[dim] < count[dim] - step
        return place[dim] >= -step

    def device(dim, step):
        return tuple(p + (step if i == dim else 0) for i, p in enumerate(place))

    peers = [(0, k) for k in (1, -1, 2, -2, 3, -3)] + [(1, 1), (1, -1), (2, 1), (2, -1)]
    barrier = pltpu.get_barrier_semaphore()
    for dim, step in reversed(peers):

        @pl.when(exists(dim, step))
        def _():
            pl.semaphore_signal(barrier, inc=1, device_id=device(dim, step), device_id_type=MESH)

    loads = []
    for a, ref in enumerate((s_hbm, c_hbm)):
        load = pltpu.make_async_copy(ref, e1.at[a, 3:11, 8:40, :], in_sem.at[a])
        load.start()
        loads.append(load)
    for load in loads:
        load.wait()

    for a in range(2):
        for k in range(4):
            sums2[a, k] = sum(e1[a, 3 + 2 * k + dz, pl.ds(8 + dy, 16, stride=2), :] for dz in range(2) for dy in range(2))
        for k in range(2):
            sums3[a, k] = sum(sums2[a, 2 * k + dz, pl.ds(dy, 8, stride=2), :] for dz in range(2) for dy in range(2))
        deep = sum(sums3[a, dz, pl.ds(dy, 4, stride=2), :] for dz in range(2) for dy in range(2))
        sums4[a, 0, 0:4] = deep
        sums4[a, 0, 4:8] = deep
    for level, sums in ((1, sums2), (2, sums3), (3, sums4)):
        shape = sums.shape
        pick = jnp.where((iota((LANES, LANES), 0) >> level) == iota((LANES, LANES), 1), 0.125**level, 0.0)
        rows = sums[...].reshape(-1, LANES)
        mean = jnp.dot(rows, pick, precision=EXACT, preferred_element_type=jnp.float32).reshape(shape)
        d = DEPTH[level]
        ext[level][:, 3 : 3 + d, 8 : 8 + SENT[level], :] = mean

    expected = 0
    for dim, step in peers:
        expected = expected + jnp.where(exists(dim, step), 1, 0)
    pl.semaphore_wait(barrier, expected)

    def go(copies):
        for copy, to, _ in copies:
            pl.when(to)(copy.start)

    def landed(copies):
        for copy, _, fro in copies:
            pl.when(fro)(copy.wait_recv)

    def left(copies):
        for copy, to, _ in copies:
            pl.when(to)(copy.wait_send)

    copies = []
    for step in (1, -1, 2, -2, 3, -3):
        for level in range(4):
            d = DEPTH[level]
            if step > 0:
                first, last = max(0, step * d - HALO), d
            else:
                first, last = 0, min(d, HALO + step * d + d)
            if first >= last:
                continue
            at = 3 + first - step * d
            rows = slice(8, 8 + SENT[level])
            n = len(copies)
            copy = pltpu.make_async_remote_copy(
                src_ref=ext[level].at[:, 3 + first : 3 + last, rows, :],
                dst_ref=ext[level].at[:, at : at + last - first, rows, :],
                send_sem=zs.at[n],
                recv_sem=zr.at[n],
                device_id=device(0, step),
                device_id_type=MESH,
            )
            copies.append((copy, exists(0, step), exists(0, -step)))
    go(copies)
    landed(copies)
    sent = copies

    copies = []
    for step in (1, -1):
        for level in range(4):
            low, high, end = 8, SENT[level], 8 + SENT[level]
            src = high if step > 0 else low
            dst = 0 if step > 0 else end
            n = len(copies)
            copy = pltpu.make_async_remote_copy(
                src_ref=ext[level].at[:, :, src : src + 8, :],
                dst_ref=ext[level].at[:, :, dst : dst + 8, :],
                send_sem=ys.at[n],
                recv_sem=yr.at[n],
                device_id=device(1, step),
                device_id_type=MESH,
            )
            copies.append((copy, exists(1, step), exists(1, -step)))
    go(copies)
    landed(copies)
    sent = sent + copies

    for level in range(4):
        tall = 16 if level == 3 else TALL[level]
        lane = iota((tall, LANES), 1)
        packs = [jnp.zeros((tall, LANES), jnp.float32)] * 2
        for z in range(DEPTH[level] + 2 * HALO):
            for a in range(2):
                at = LANE0[level] + 6 * z + 3 * a
                here = (lane >= at) & (lane < at + 3)
                cells = extended_plane(ext, level, a, z)
                packs[0] = put(here, pltpu.roll(cells, at % LANES, 1), packs[0])
                packs[1] = put(here, pltpu.roll(cells, (at - COLS[level] + 3) % LANES, 1), packs[1])
        wide = 6 * (DEPTH[level] + 2 * HALO)
        here = (lane >= LANE0[level]) & (lane < LANE0[level] + wide)
        rows = slice(ROW0[level], ROW0[level] + tall)
        for side in range(2):
            if LANE0[level]:
                msg[side, rows] = put(here, packs[side], msg[side, rows])
            else:
                msg[side, rows] = packs[side]
    copies = []
    for side, step in ((0, -1), (1, 1)):
        copy = pltpu.make_async_remote_copy(
            src_ref=msg.at[side],
            dst_ref=got.at[1 - side],
            send_sem=xs.at[side],
            recv_sem=xr.at[side],
            device_id=device(2, step),
            device_id_type=MESH,
        )
        copies.append((copy, exists(2, step), exists(2, -step)))
    go(copies)
    landed(copies)
    left(sent + copies)


def ring_roll(chunks, shift):
    turned = [pltpu.roll(c, shift % LANES, 1) for c in chunks]
    if len(chunks) == 1:
        return turned
    lane = iota(chunks[0].shape, 1)
    edge = lane == (0 if shift > 0 else LANES - 1)
    return [put(edge, turned[1 - k], turned[k]) for k in range(2)]


def triple(planes, z):
    out = []
    for k in range(len(planes[z])):
        v = planes[z - 1][k] + 2.0 * planes[z][k] + planes[z + 1][k]
        n = v.shape[0]
        out.append(pltpu.roll(v, 1, 0) + 2.0 * v + pltpu.roll(v, n - 1, 0))
    before, after = ring_roll(out, 1), ring_roll(out, -1)
    return [b + 2.0 * v + f for b, v, f in zip(before, out, after)]


def cycle(e1, e2, e3, e4, got, corr_ref, res_ref, *spread):
    ext = (e1, e2, e3, e4)
    place = tuple(lax.axis_index(a) for a in AXES)
    count = tuple(lax.axis_size(a) for a in AXES)
    solved, sources, centres = [], [], []
    for level in range(4):
        d, rows, cols = DEPTH[level], ROWS[level], COLS[level]
        tall = 16 if level == 3 else TALL[level]
        lane, row = iota((tall, LANES), 1), iota((tall, LANES), 0)
        y = row - 8
        y_all = place[1] * rows + y
        y_ok = (y >= -HALO) & (y < rows + HALO) & (y_all >= 0) & (y_all < count[1] * rows)
        near = lane < cols
        right = (lane >= cols % LANES) & (lane < cols % LANES + HALO)
        leftward = lane >= LANES - HALO
        side_ok = (right & (place[2] < count[2] - 1)) | (leftward & (place[2] > 0))
        oks = [y_ok, y_ok & side_ok] if level == 0 else [y_ok & (near | side_ok)]
        src, cen, inv = [], [], []
        for z in range(d + 2 * HALO):
            z_all = place[0] * d + z - HALO
            z_ok = (z_all >= 0) & (z_all < count[0] * d)
            both = []
            for a in range(2):
                at = LANE0[level] + 6 * z + 3 * a
                strip = slice(ROW0[level], ROW0[level] + tall)
                main = extended_plane(ext, level, a, z)
                from_left = pltpu.roll(got[0, strip], (LANES - HALO - at) % LANES, 1)
                from_right = pltpu.roll(got[1, strip], (cols - at) % LANES, 1)
                if level == 0:
                    both.append([main, put(leftward, from_left, from_right)])
                else:
                    both.append([put(near, main, put(leftward, from_left, from_right))])
            oks_z = [ok & z_ok for ok in oks]
            src.append([put(ok, v, 0.0) for ok, v in zip(oks_z, both[0])])
            coef = [put(ok, v, 0.0) for ok, v in zip(oks_z, both[1])]
            cen.append([v + 16.0 for v in coef])
            inv.append([put(ok, 1.0 / (v + 14.0), 0.0) for ok, v in zip(oks_z, coef)])
        planes = [[TAUS[0] * s * i for s, i in zip(sz, iz)] for sz, iz in zip(src, inv)]
        for k in (1, 2):
            new = [None] * len(planes)
            for z in range(k, len(planes) - k):
                around = triple(planes, z)
                new[z] = [x + TAUS[k] * (s - m * x + 0.25 * t) * i for x, s, m, t, i in zip(planes[z], src[z], cen[z], around, inv[z])]
            planes = new
        solved.append(planes)
        sources.append(src)
        centres.append(cen)

    total = solved[3]
    for level in (2, 1, 0):
        tall = TALL[level]
        width = 2 * LANES if level == 0 else LANES
        col = iota((LANES, width), 1)
        col = put(col >= width - width // 4, col - width, col)
        pick = jnp.where(((col >> 1) & (LANES - 1)) == iota((LANES, width), 0), 1.0, 0.0)
        buf, wide = spread[2 * level], spread[2 * level + 1]
        coarse = DEPTH[level + 1]
        for n in range(coarse + 2):
            buf[n] = total[n + 2][0]
        for n in range(coarse + 2):
            half = buf[n, 4 : 4 + tall // 2, :]
            half = jnp.dot(half, pick, precision=EXACT, preferred_element_type=jnp.float32)
            for dy in range(2):
                for k in range(width // LANES):
                    wide[n, k, pl.ds(dy, tall // 2, stride=2), :] = half[:, k * LANES : (k + 1) * LANES]
        new = [None] * len(solved[level])
        share = 0.5 if level == 0 else 1.0
        for z in range(-1, DEPTH[level] + 1):
            n = (z >> 1) + 1
            new[z + 3] = [x + share * wide[n, k] for k, x in enumerate(solved[level][z + 3])]
        total = new
    for z in range(8):
        corr_ref[z] = total[z + 3][0][8:40]
        around = triple(total, z + 3)[0]
        res = sources[0][z + 3][0] - centres[0][z + 3][0] * total[z + 3][0] + 0.25 * around
        res_ref[z] = res[8:40]


def per_device(right_side, reaction):
    f32 = jnp.float32
    vmem = pl.BlockSpec(memory_space=pltpu.VMEM)
    shapes = [jax.ShapeDtypeStruct((2, d + 2 * HALO, t, LANES), f32) for d, t in zip(DEPTH, TALL)]
    shapes.append(jax.ShapeDtypeStruct((2, MSG_ROWS, LANES), f32))
    extended = pl.pallas_call(
        exchange,
        out_shape=shapes,
        in_specs=[pl.BlockSpec(memory_space=pl.ANY)] * 2,
        out_specs=[vmem] * 5,
        scratch_shapes=[
            pltpu.VMEM((2, 4, 16, LANES), f32),
            pltpu.VMEM((2, 2, 8, LANES), f32),
            pltpu.VMEM((2, 1, 8, LANES), f32),
            pltpu.VMEM((2, MSG_ROWS, LANES), f32),
            pltpu.SemaphoreType.DMA((2,)),
            pltpu.SemaphoreType.DMA((16,)),
            pltpu.SemaphoreType.DMA((16,)),
            pltpu.SemaphoreType.DMA((8,)),
            pltpu.SemaphoreType.DMA((8,)),
            pltpu.SemaphoreType.DMA((2,)),
            pltpu.SemaphoreType.DMA((2,)),
        ],
        compiler_params=pltpu.CompilerParams(collective_id=0, has_side_effects=True, vmem_limit_bytes=32 * 1024 * 1024),
    )(right_side, reaction)
    block = jax.ShapeDtypeStruct(right_side.shape, f32)
    spread = []
    for level in (0, 1, 2):
        coarse_tall = 16 if level == 2 else TALL[level + 1]
        n = DEPTH[level + 1] + 2
        spread.append(pltpu.VMEM((n, coarse_tall, LANES), f32))
        spread.append(pltpu.VMEM((n, 2 if level == 0 else 1, TALL[level], LANES), f32))
    return pl.pallas_call(
        cycle,
        out_shape=[block, block],
        in_specs=[vmem] * 5,
        out_specs=[vmem] * 2,
        scratch_shapes=spread,
        compiler_params=pltpu.CompilerParams(vmem_limit_bytes=32 * 1024 * 1024),
    )(*extended)


def solution(mesh):
    spec = P(*AXES)
    return jax.shard_map(
        lambda s, c: tuple(per_device(s, c)),
        mesh=mesh,
        in_specs=(spec, spec),
        out_specs=(spec, spec),
        check_vma=False,
    )
```

time: 422 us -> 43.9 us (0.10)
  the two profiles are of different devices: /device:TPU:40 before, /device:TPU:43 now
where the time goes in v1:
time: 43.9 us; the launch traced here: 43.7 us
  Pallas kernels  41.3 us (94%)
  local copies, waits for them, and re-layouts  1.8 us (4%)
  between operations  0.65 us (1%)
    pallas_call x1, Pallas kernels, per_device(): pl.pallas_call(exchange, out_shape=shapes, in_specs=[pl.BlockSpec(memory_...  37.8 us
    pallas_call x1, Pallas kernels, per_device(): pl.pallas_call(cycle, out_shape=[block, block], in_specs=[vmem] * 5, out_...  3.44 us
    unnamed x4, local copies, waits for them, and re-layouts  1.8 us

profile of v1, /device:TPU:43, one launch (start us, length us, event | category | flops | bytes accessed | tf_op | source)
XLA Modules:
  0.0 43.7 jit_solution(5421218022751388402)
XLA Ops:
  0.6 0.0 copy-start
  0.6 0.9 %copy-done = f32[8,32,128]{2,1,0:T(8,128)S(1)} copy-done((f32[8,32,128]{2,1,0:T(8,128)S(1)}, f32[8,32,128]{2,1,0:T(8,128)}, u32[]{:S(2)}) %copy-start) | copy-done | bytes 131096
  1.5 0.0 copy-start.1
  1.5 0.9 %copy-done.1 = f32[8,32,128]{2,1,0:T(8,128)S(1)} copy-done((f32[8,32,128]{2,1,0:T(8,128)S(1)}, f32[8,32,128]{2,1,0:T(8,128)}, u32[]{:S(2)}) %copy-start.1) | copy-done | bytes 131096
  2.4 37.8 %shard_map.41 = (f32[2,14,48,128]{3,2,1,0:T(8,128)S(1)}, f32[2,10,32,128]{3,2,1,0:T(8,128)S(1)}, f32[2,8,24,128]{3,2,1,0:T(8,128)S(1)}, f32[2,7,24,128]{3,2,1,0:T(8,128)S(1)}, f32[2,80,128]{2,1,0:T(8,128)S(1)}) custom-call(f32[8,32,128]{2,1,0:T(8,128)S(1)} %copy-done, f32[8,32,128]{2,1,0:T(8,128)S(1)} %copy-done.1), custom_call_target="tpu_custom_call" | custom-call | tf_op jit(solution)/shard_map/pallas_call | solution.py:287
  40.3 3.4 %shard_map.42 = (f32[8,32,128]{2,1,0:T(8,128)}, f32[8,32,128]{2,1,0:T(8,128)}) custom-call(f32[2,14,48,128]{3,2,1,0:T(8,128)S(1)} %get-tuple-element.7.e1, f32[2,10,32,128]{3,2,1,0:T(8,128)S(1)} %get-tuple-element.8.e2, f32[2,8,24,128]{3,2,1,0:T(8,128)S(1)} %get-tuple-element.9.e3, f32[2,7,24,128]{3,2,1,0:T(8,128)S(1)} %get-tuple-element.10.e4, ...), custom_call_target="tpu_custom_call" | custom-call | tf_op jit(solution)/shard_map/pallas_call | solution.py:314
Async XLA Ops:
  0.6 0.9 %copy-start = (f32[8,32,128]{2,1,0:T(8,128)S(1)}, f32[8,32,128]{2,1,0:T(8,128)}, u32[]{:S(2)}) copy-start(f32[8,32,128]{2,1,0:T(8,128)} %s_hbm.1) | copy-start | bytes 393220
  1.5 0.9 %copy-start.1 = (f32[8,32,128]{2,1,0:T(8,128)S(1)}, f32[8,32,128]{2,1,0:T(8,128)}, u32[]{:S(2)}) copy-start(f32[8,32,128]{2,1,0:T(8,128)} %c_hbm.1) | copy-start | bytes 393220

commit v2 on v1

v2 whole, which is shorter than its diff:
```python
import functools
import math

import jax
import jax.numpy as jnp
from jax import lax
from jax.experimental import pallas as pl
from jax.experimental.pallas import tpu as pltpu
from jax.sharding import PartitionSpec as P

MESH = pl.DeviceIdType.MESH
AXES = ("grp", "gy", "gx")
TAUS = tuple(1.0 / (1.15 + 0.85 * math.cos((2 * k - 1) * math.pi / 6.0)) for k in (1, 2, 3))
EXACT = lax.Precision.HIGHEST
LANES = 128
HALO = 3
DEPTH = (8, 4, 2, 1)
ROWS = (32, 16, 8, 4)
COLS = (128, 64, 32, 16)
TALL = (48, 32, 24, 16)
NEAR = tuple((dz, dy) for dz in (-1, 0, 1) for dy in (-1, 0, 1) if dz or dy)
FAR = tuple((dz, dy) for dz in (-3, 3, -2, 2) for dy in (-1, 0, 1))


def iota(shape, dim):
    return lax.broadcasted_iota(jnp.int32, shape, dim)


def put(cond, value, other):
    return jnp.where(cond, value, other)


def exchange(s_hbm, c_hbm, fine, second, deep, strips, sums2, sums3, sums4, msg, in_sem, xs, xr, bs, br, fs, fr):
    place = tuple(lax.axis_index(a) for a in AXES)
    count = tuple(lax.axis_size(a) for a in AXES)

    def exists(*steps):
        ok = True
        for p, n, step in zip(place, count, steps):
            if step > 0:
                ok = ok & (p < n - step)
            if step < 0:
                ok = ok & (p >= -step)
        return ok

    def device(*steps):
        return tuple(p + step for p, step in zip(place, steps))

    peers = [(0, 0, -1), (0, 0, 1)] + [(dz, dy, 0) for dz, dy in FAR + NEAR]
    barrier = pltpu.get_barrier_semaphore()
    for peer in peers:

        @pl.when(exists(*peer))
        def _():
            pl.semaphore_signal(barrier, inc=1, device_id=device(*peer), device_id_type=MESH)

    loads = []
    for a, ref in enumerate((s_hbm, c_hbm)):
        load = pltpu.make_async_copy(ref, fine.at[a, 3:11, 8:40, :], in_sem.at[a])
        load.start()
        loads.append(load)
    for load in loads:
        load.wait()

    for a in range(2):
        for k in range(4):
            sums2[a, k] = sum(fine[a, 3 + 2 * k + dz, pl.ds(8 + dy, 16, stride=2), :] for dz in range(2) for dy in range(2))
        for k in range(2):
            sums3[a, k] = sum(sums2[a, 2 * k + dz, pl.ds(dy, 8, stride=2), :] for dz in range(2) for dy in range(2))
        last = sum(sums3[a, dz, pl.ds(dy, 4, stride=2), :] for dz in range(2) for dy in range(2))
        sums4[a, 0:4] = last
        sums4[a, 4:8] = last

    def mean(level, rows, first):
        pick = jnp.where((iota((LANES, LANES), 0) >> level) + first == iota((LANES, LANES), 1), 0.125**level, 0.0)
        return jnp.dot(rows, pick, precision=EXACT, preferred_element_type=jnp.float32)

    level2 = sum(mean(1, sums2[a].reshape(64, LANES), 64 * a) for a in range(2))
    second[3:7, 8:24, :] = level2.reshape(4, 16, LANES)
    level3 = sum(mean(2, sums3[a].reshape(16, LANES), 32 * a) for a in range(2)).reshape(2, 8, LANES)
    level4 = sum(mean(3, sums4[a], 64 + 16 * a) for a in range(2))
    deep[3, 1] = level3 + level4[None]

    def gather(parts, rows):
        lane = iota((rows, LANES), 1)
        packs = [jnp.zeros((rows, LANES), jnp.float32)] * 2
        for cells, at, first, cols in parts:
            here = (lane >= at) & (lane < at + HALO)
            packs[0] = put(here, pltpu.roll(cells, (at - first) % LANES, 1), packs[0])
            packs[1] = put(here, pltpu.roll(cells, (at - first - cols + HALO) % LANES, 1), packs[1])
        return packs

    parts = []
    for a in range(2):
        for z in range(8):
            for half in range(2):
                cells = fine[a, 3 + z, 8 + 16 * half : 24 + 16 * half]
                parts.append((cells, 48 * half + 6 * z + 3 * a, 0, 128))
        for z in range(4):
            parts.append((second[3 + z, 8:24], 96 + 6 * z + 3 * a, 64 * a, 64))
    upper = gather(parts, 16)
    parts = []
    for a in range(2):
        for z in range(2):
            parts.append((deep[3, 1, z], 6 * z + 3 * a, 32 * a, 32))
        parts.append((deep[3, 1, 0], 12 + 3 * a, 64 + 16 * a, 16))
    lower = gather(parts, 8)
    for side in range(2):
        msg[side, 0:8] = upper[side][0:8]
        msg[side, 8:16] = lower[side]
        msg[side, 16:24] = upper[side][8:16]

    expected = 0
    for peer in peers:
        expected = expected + jnp.where(exists(*peer), 1, 0)
    pl.semaphore_wait(barrier, expected)

    def remote(src, dst, sems, n, *peer):
        copy = pltpu.make_async_remote_copy(
            src_ref=src, dst_ref=dst, send_sem=sems[0].at[n], recv_sem=sems[1].at[n], device_id=device(*peer), device_id_type=MESH
        )
        pl.when(exists(*peer))(copy.start)
        return copy, exists(*peer), exists(*(-step for step in peer))

    def landed(copies):
        for copy, _, fro in copies:
            pl.when(fro)(copy.wait_recv)

    across = [remote(msg.at[side], strips.at[3, 1, 1 - side], (xs, xr), side, 0, 0, 2 * side - 1) for side in range(2)]

    blocks = []
    for dz, dy in NEAR + FAR:
        for ref, depth, rows in ((fine, 8, 32), (second, 4, 16)):
            if abs(dz) > 1:
                continue
            z0, z1 = {-1: (3, 6), 0: (3, 3 + depth), 1: (depth, 3 + depth)}[dz]
            y0, y1 = {-1: (8, 16), 0: (8, 8 + rows), 1: (rows, 8 + rows)}[dy]
            up, along = z0 - dz * depth, y0 - dy * rows
            src, dst = ref, ref
            if ref is fine:
                src, dst = fine.at[:, z0:z1, y0:y1, :], fine.at[:, up : up + z1 - z0, along : along + y1 - y0, :]
            else:
                src, dst = second.at[z0:z1, y0:y1, :], second.at[up : up + z1 - z0, along : along + y1 - y0, :]
            blocks.append(remote(src, dst, (bs, br), len(blocks), dz, dy, 0))
        blocks.append(remote(deep.at[3, 1], deep.at[3 - dz, 1 - dy], (bs, br), len(blocks), dz, dy, 0))

    landed(across)
    passed = []
    for dz, dy in FAR + NEAR:
        rows = slice(8, 16) if abs(dz) > 1 else {-1: slice(0, 16), 0: slice(0, 24), 1: slice(8, 24)}[dy]
        passed.append(remote(strips.at[3, 1, :, rows, :], strips.at[3 - dz, 1 - dy, :, rows, :], (fs, fr), len(passed), dz, dy, 0))
    landed(blocks + passed)
    for copy, to, _ in across + blocks + passed:
        pl.when(to)(copy.wait_send)


def ring_roll(chunks, shift):
    turned = [pltpu.roll(c, shift % LANES, 1) for c in chunks]
    if len(chunks) == 1:
        return turned
    lane = iota(chunks[0].shape, 1)
    edge = lane == (0 if shift > 0 else LANES - 1)
    return [put(edge, turned[1 - k], turned[k]) for k in range(2)]


def triple(planes, z):
    out = []
    for k in range(len(planes[z])):
        v = planes[z - 1][k] + 2.0 * planes[z][k] + planes[z + 1][k]
        n = v.shape[0]
        out.append(pltpu.roll(v, 1, 0) + 2.0 * v + pltpu.roll(v, n - 1, 0))
    before, after = ring_roll(out, 1), ring_roll(out, -1)
    return [b + 2.0 * v + f for b, v, f in zip(before, out, after)]


def columns(strips, level, a, z, side, first):
    dz, p = z // DEPTH[level], z % DEPTH[level]

    def tiles(dy, lane, *which):
        rows = [strips[dz + 3, dy + 1, side, 8 * t : 8 * t + 8] for t in which]
        rows = rows[0] if len(rows) == 1 else jnp.concatenate(rows, axis=0)
        return pltpu.roll(rows, (first - lane) % LANES, 1)

    if level == 0:
        low, high = 6 * p + 3 * a, 48 + 6 * p + 3 * a
        pieces = [tiles(-1, high, 2), tiles(0, low, 0, 2), tiles(0, high, 0, 2), tiles(1, low, 0)]
    elif level == 1:
        at = 96 + 6 * p + 3 * a
        pieces = [tiles(-1, at, 2), tiles(0, at, 0, 2), tiles(1, at, 0)]
    else:
        at = 6 * p + 3 * a if level == 2 else 12 + 3 * a
        pieces = [tiles(dy, at, 1) for dy in (-1, 0, 1)]
        if level == 3:
            pieces = [pieces[0], put(iota((8, LANES), 0) < 4, pieces[1], pieces[2])]
    return jnp.concatenate(pieces, axis=0)


def own(fine, second, deep, level, a, z):
    if level == 0:
        return fine[a, z + 3]
    if level == 1:
        return pltpu.roll(second[z + 3], 64, 1) if a else second[z + 3]
    dz, p = z // DEPTH[level], z % DEPTH[level]
    pieces = [deep[dz + 3, dy, p] for dy in range(3)]
    if level == 3:
        pieces = [pieces[0], put(iota((8, LANES), 0) < 4, pieces[1], pieces[2])]
    cells = jnp.concatenate(pieces, axis=0)
    first = 32 * a if level == 2 else 64 + 16 * a
    return pltpu.roll(cells, (-first) % LANES, 1) if first else cells


def cycle(fine, second, deep, strips, corr_ref, res_ref, *spread):
    place = tuple(lax.axis_index(a) for a in AXES)
    count = tuple(lax.axis_size(a) for a in AXES)
    solved, sources, centres = [], [], []
    for level in range(4):
        d, rows, cols, tall = DEPTH[level], ROWS[level], COLS[level], TALL[level]
        lane, row = iota((tall, LANES), 1), iota((tall, LANES), 0)
        y = row - 8
        y_all = place[1] * rows + y
        y_ok = (y >= -HALO) & (y < rows + HALO) & (y_all >= 0) & (y_all < count[1] * rows)
        near = lane < cols
        right = (lane >= cols % LANES) & (lane < cols % LANES + HALO)
        leftward = lane >= LANES - HALO
        side_ok = (right & (place[2] < count[2] - 1)) | (leftward & (place[2] > 0))
        oks = [y_ok, y_ok & side_ok] if level == 0 else [y_ok & (near | side_ok)]
        src, cen, inv = [], [], []
        for z in range(-HALO, d + HALO):
            z_all = place[0] * d + z
            z_ok = (z_all >= 0) & (z_all < count[0] * d)
            both = []
            for a in range(2):
                main = own(fine, second, deep, level, a, z)
                sides = put(leftward, columns(strips, level, a, z, 0, LANES - HALO), columns(strips, level, a, z, 1, cols % LANES))
                both.append([main, sides] if level == 0 else [put(near, main, sides)])
            oks_z = [ok & z_ok for ok in oks]
            src.append([put(ok, v, 0.0) for ok, v in zip(oks_z, both[0])])
            coef = [put(ok, v, 0.0) for ok, v in zip(oks_z, both[1])]
            cen.append([v + 16.0 for v in coef])
            inv.append([put(ok, 1.0 / (v + 14.0), 0.0) for ok, v in zip(oks_z, coef)])
        planes = [[TAUS[0] * s * i for s, i in zip(sz, iz)] for sz, iz in zip(src, inv)]
        for k in (1, 2):
            new = [None] * len(planes)
            for z in range(k, len(planes) - k):
                around = triple(planes, z)
                new[z] = [x + TAUS[k] * (s - m * x + 0.25 * t) * i for x, s, m, t, i in zip(planes[z], src[z], cen[z], around, inv[z])]
            planes = new
        solved.append(planes)
        sources.append(src)
        centres.append(cen)

    total = solved[3]
    for level in (2, 1, 0):
        tall = TALL[level]
        width = 2 * LANES if level == 0 else LANES
        col = iota((LANES, width), 1)
        col = put(col >= width - width // 4, col - width, col)
        pick = jnp.where(((col >> 1) & (LANES - 1)) == iota((LANES, width), 0), 1.0, 0.0)
        buf, wide = spread[2 * level], spread[2 * level + 1]
        coarse = DEPTH[level + 1]
        for n in range(coarse + 2):
            buf[n] = total[n + 2][0]
        for n in range(coarse + 2):
            half = buf[n, 4 : 4 + tall // 2, :]
            half = jnp.dot(half, pick, precision=EXACT, preferred_element_type=jnp.float32)
            for dy in range(2):
                for k in range(width // LANES):
                    wide[n, k, pl.ds(dy, tall // 2, stride=2), :] = half[:, k * LANES : (k + 1) * LANES]
        new = [None] * len(solved[level])
        share = 0.5 if level == 0 else 1.0
        for z in range(-1, DEPTH[level] + 1):
            n = (z >> 1) + 1
            new[z + 3] = [x + share * wide[n, k] for k, x in enumerate(solved[level][z + 3])]
        total = new
    for z in range(8):
        corr_ref[z] = total[z + 3][0][8:40]
        around = triple(total, z + 3)[0]
        res = sources[0][z + 3][0] - centres[0][z + 3][0] * total[z + 3][0] + 0.25 * around
        res_ref[z] = res[8:40]


def per_device(right_side, reaction):
    f32 = jnp.float32
    vmem = pl.BlockSpec(memory_space=pltpu.VMEM)
    shapes = [(2, 14, 48, LANES), (10, 32, LANES), (7, 3, 2, 8, LANES), (7, 3, 2, 24, LANES)]
    dma = pltpu.SemaphoreType.DMA
    blocks = 3 * len(NEAR) + len(FAR)
    extended = pl.pallas_call(
        exchange,
        out_shape=[jax.ShapeDtypeStruct(shape, f32) for shape in shapes],
        in_specs=[pl.BlockSpec(memory_space=pltpu.HBM)] * 2,
        out_specs=[vmem] * 4,
        scratch_shapes=[
            pltpu.VMEM((2, 4, 16, LANES), f32),
            pltpu.VMEM((2, 2, 8, LANES), f32),
            pltpu.VMEM((2, 8, LANES), f32),
            pltpu.VMEM((2, 24, LANES), f32),
            dma((2,)),
            dma((2,)),
            dma((2,)),
            dma((blocks,)),
            dma((blocks,)),
            dma((20,)),
            dma((20,)),
        ],
        compiler_params=pltpu.CompilerParams(collective_id=0, has_side_effects=True, vmem_limit_bytes=16 * 1024 * 1024),
    )(right_side, reaction)
    block = jax.ShapeDtypeStruct(right_side.shape, f32)
    spread = []
    for level in (0, 1, 2):
        n = DEPTH[level + 1] + 2
        spread.append(pltpu.VMEM((n, TALL[level + 1], LANES), f32))
        spread.append(pltpu.VMEM((n, 2 if level == 0 else 1, TALL[level], LANES), f32))
    return pl.pallas_call(
        cycle,
        out_shape=[block, block],
        in_specs=[vmem] * 4,
        out_specs=[vmem] * 2,
        scratch_shapes=spread,
        compiler_params=pltpu.CompilerParams(vmem_limit_bytes=16 * 1024 * 1024),
    )(*extended)


def solution(mesh):
    spec = P(*AXES)
    return jax.shard_map(
        lambda s, c: tuple(per_device(s, c)),
        mesh=mesh,
        in_specs=(spec, spec),
        out_specs=(spec, spec),
        check_vma=False,
    )
```

time: 43.9 us -> 37.1 us (0.85)
  the two profiles are of different devices: /device:TPU:43 before, /device:TPU:1 now
where the time goes in v2:
time: 37.1 us; the launch traced here: 36.5 us
  Pallas kernels  34.1 us (92%)
  local copies, waits for them, and re-layouts  1.8 us (5%)
  between operations  0.65 us (2%)
    pallas_call x1, Pallas kernels, per_device(): pl.pallas_call(exchange, out_shape=[jax.ShapeDtypeStruct(shape, f32) for...  30.4 us
    pallas_call x1, Pallas kernels, per_device(): pl.pallas_call(cycle, out_shape=[block, block], in_specs=[vmem] * 4, out_...  3.73 us
    unnamed x4, local copies, waits for them, and re-layouts  1.8 us

profile of v2, /device:TPU:1, one launch (start us, length us, event | category | flops | bytes accessed | tf_op | source)
XLA Modules:
  0.0 36.5 jit_solution(6084823474635187048)
XLA Ops:
  0.6 0.0 copy-start
  0.6 0.9 %copy-done = f32[8,32,128]{2,1,0:T(8,128)S(1)} copy-done((f32[8,32,128]{2,1,0:T(8,128)S(1)}, f32[8,32,128]{2,1,0:T(8,128)}, u32[]{:S(2)}) %copy-start) | copy-done | bytes 131096
  1.5 0.0 copy-start.1
  1.5 0.9 %copy-done.1 = f32[8,32,128]{2,1,0:T(8,128)S(1)} copy-done((f32[8,32,128]{2,1,0:T(8,128)S(1)}, f32[8,32,128]{2,1,0:T(8,128)}, u32[]{:S(2)}) %copy-start.1) | copy-done | bytes 131096
  2.4 30.4 %shard_map.41 = (f32[2,14,48,128]{3,2,1,0:T(8,128)S(1)}, f32[10,32,128]{2,1,0:T(8,128)S(1)}, f32[7,3,2,8,128]{4,3,2,1,0:T(8,128)S(1)}, f32[7,3,2,24,128]{4,3,2,1,0:T(8,128)S(1)}) custom-call(f32[8,32,128]{2,1,0:T(8,128)S(1)} %copy-done, f32[8,32,128]{2,1,0:T(8,128)S(1)} %copy-done.1), custom_call_target="tpu_custom_call" | custom-call | tf_op jit(solution)/shard_map/pallas_call | solution.py:288
  32.8 3.7 %shard_map.42 = (f32[8,32,128]{2,1,0:T(8,128)}, f32[8,32,128]{2,1,0:T(8,128)}) custom-call(f32[2,14,48,128]{3,2,1,0:T(8,128)S(1)} %get-tuple-element.6.fine, f32[10,32,128]{2,1,0:T(8,128)S(1)} %get-tuple-element.7.second, f32[7,3,2,8,128]{4,3,2,1,0:T(8,128)S(1)} %get-tuple-element.8.deep, f32[7,3,2,24,128]{4,3,2,1,0:T(8,128)S(1)} %get-tuple-element.9.strips), custom_call_target="tpu_custom_call" | custom-call | tf_op jit(solution)/shard_map/pallas_call | solution.py:314
Async XLA Ops:
  0.6 0.9 %copy-start = (f32[8,32,128]{2,1,0:T(8,128)S(1)}, f32[8,32,128]{2,1,0:T(8,128)}, u32[]{:S(2)}) copy-start(f32[8,32,128]{2,1,0:T(8,128)} %s_hbm.1) | copy-start | bytes 393220
  1.5 0.9 %copy-start.1 = (f32[8,32,128]{2,1,0:T(8,128)S(1)}, f32[8,32,128]{2,1,0:T(8,128)}, u32[]{:S(2)}) copy-start(f32[8,32,128]{2,1,0:T(8,128)} %c_hbm.1) | copy-start | bytes 393220

commit v3 on v2

--- a/solution.py
+++ b/solution.py
@@ -30,6 +30,21 @@
     return jnp.where(cond, value, other)
 
 
+def slide(cells, width):
+    row = iota(cells.shape, 0)
+    for k in (1, 2, 4):
+        cells = put(row & k != 0, pltpu.roll(cells, k * width % LANES, 1), cells)
+    return cells
+
+
+def in_row(cells, width):
+    return jnp.sum(slide(cells, width), axis=0, keepdims=True)
+
+
+def off_row(row, width):
+    return slide(jnp.broadcast_to(row, (8, LANES)), LANES - width)
+
+
 def exchange(s_hbm, c_hbm, fine, second, deep, strips, sums2, sums3, sums4, msg, in_sem, xs, xr, bs, br, fs, fr):
     place = tuple(lax.axis_index(a) for a in AXES)
     count = tuple(lax.axis_size(a) for a in AXES)
@@ -69,7 +84,7 @@
             sums3[a, k] = sum(sums2[a, 2 * k + dz, pl.ds(dy, 8, stride=2), :] for dz in range(2) for dy in range(2))
         last = sum(sums3[a, dz, pl.ds(dy, 4, stride=2), :] for dz in range(2) for dy in range(2))
         sums4[a, 0:4] = last
-        sums4[a, 4:8] = last
+        sums4[a, 4:8] = jnp.zeros_like(last)
 
     def mean(level, rows, first):
         pick = jnp.where((iota((LANES, LANES), 0) >> level) + first == iota((LANES, LANES), 1), 0.125**level, 0.0)
@@ -77,9 +92,10 @@
 
     level2 = sum(mean(1, sums2[a].reshape(64, LANES), 64 * a) for a in range(2))
     second[3:7, 8:24, :] = level2.reshape(4, 16, LANES)
-    level3 = sum(mean(2, sums3[a].reshape(16, LANES), 32 * a) for a in range(2)).reshape(2, 8, LANES)
-    level4 = sum(mean(3, sums4[a], 64 + 16 * a) for a in range(2))
-    deep[3, 1] = level3 + level4[None]
+    level3 = sum(mean(2, sums3[a, z], 64 * z + 32 * a) for a in range(2) for z in range(2))
+    level4 = in_row(sum(mean(3, sums4[a], 16 * a) for a in range(2)), 32)
+    deep[3, 1, 0:8] = level3
+    deep[3, 1, 8:9] = level4
 
     def gather(parts, rows):
         lane = iota((rows, LANES), 1)
@@ -102,13 +118,15 @@
     parts = []
     for a in range(2):
         for z in range(2):
-            parts.append((deep[3, 1, z], 6 * z + 3 * a, 32 * a, 32))
-        parts.append((deep[3, 1, 0], 12 + 3 * a, 64 + 16 * a, 16))
+            parts.append((level3, 6 * z + 3 * a, 64 * z + 32 * a, 32))
     lower = gather(parts, 8)
+    last = off_row(level4, 32)
+    last = gather([(last, 3 * a, 16 * a, 16) for a in range(2)], 8)
     for side in range(2):
-        msg[side, 0:8] = upper[side][0:8]
-        msg[side, 8:16] = lower[side]
-        msg[side, 16:24] = upper[side][8:16]
+        msg[side, 0:8] = upper[side][8:16]
+        msg[side, 8:9] = in_row(lower[side], 16)
+        msg[side, 9:10] = in_row(last[side], 16)
+        msg[side, 10:18] = upper[side][0:8]
 
     expected = 0
     for peer in peers:
@@ -126,7 +144,7 @@
         for copy, _, fro in copies:
             pl.when(fro)(copy.wait_recv)
 
-    across = [remote(msg.at[side], strips.at[3, 1, 1 - side], (xs, xr), side, 0, 0, 2 * side - 1) for side in range(2)]
+    across = [remote(msg.at[side, 0:18], strips.at[3, 1, 1 - side, 0:18], (xs, xr), side, 0, 0, 2 * side - 1) for side in range(2)]
 
     blocks = []
     for dz, dy in NEAR + FAR:
@@ -134,7 +152,7 @@
             if abs(dz) > 1:
                 continue
             z0, z1 = {-1: (3, 6), 0: (3, 3 + depth), 1: (depth, 3 + depth)}[dz]
-            y0, y1 = {-1: (8, 16), 0: (8, 8 + rows), 1: (rows, 8 + rows)}[dy]
+            y0, y1 = {-1: (8, 11), 0: (8, 8 + rows), 1: (rows + 5, rows + 8)}[dy]
             up, along = z0 - dz * depth, y0 - dy * rows
             src, dst = ref, ref
             if ref is fine:
@@ -142,12 +160,13 @@
             else:
                 src, dst = second.at[z0:z1, y0:y1, :], second.at[up : up + z1 - z0, along : along + y1 - y0, :]
             blocks.append(remote(src, dst, (bs, br), len(blocks), dz, dy, 0))
-        blocks.append(remote(deep.at[3, 1], deep.at[3 - dz, 1 - dy], (bs, br), len(blocks), dz, dy, 0))
+        rows = slice(8, 9) if abs(dz) == 3 else slice(0, 9)
+        blocks.append(remote(deep.at[3, 1, rows], deep.at[3 - dz, 1 - dy, rows], (bs, br), len(blocks), dz, dy, 0))
 
     landed(across)
     passed = []
     for dz, dy in FAR + NEAR:
-        rows = slice(8, 16) if abs(dz) > 1 else {-1: slice(0, 16), 0: slice(0, 24), 1: slice(8, 24)}[dy]
+        rows = slice(8, 10) if abs(dz) > 1 else {-1: slice(8, 13), 0: slice(0, 18), 1: slice(5, 10)}[dy]
         passed.append(remote(strips.at[3, 1, :, rows, :], strips.at[3 - dz, 1 - dy, :, rows, :], (fs, fr), len(passed), dz, dy, 0))
     landed(blocks + passed)
     for copy, to, _ in across + blocks + passed:
@@ -173,46 +192,52 @@
     return [b + 2.0 * v + f for b, v, f in zip(before, out, after)]
 
 
-def columns(strips, level, a, z, side, first):
+def columns(strips, level, a, z, side, first, seen):
     dz, p = z // DEPTH[level], z % DEPTH[level]
 
     def tiles(dy, lane, *which):
-        rows = [strips[dz + 3, dy + 1, side, 8 * t : 8 * t + 8] for t in which]
+        rows = [strips[dz + 3, dy + 1, side, 10:18] if t == 0 else strips[dz + 3, dy + 1, side, 0:8] for t in which]
         rows = rows[0] if len(rows) == 1 else jnp.concatenate(rows, axis=0)
         return pltpu.roll(rows, (first - lane) % LANES, 1)
 
     if level == 0:
         low, high = 6 * p + 3 * a, 48 + 6 * p + 3 * a
-        pieces = [tiles(-1, high, 2), tiles(0, low, 0, 2), tiles(0, high, 0, 2), tiles(1, low, 0)]
+        pieces = [tiles(-1, high, 1), tiles(0, low, 0, 1), tiles(0, high, 0, 1), tiles(1, low, 0)]
     elif level == 1:
         at = 96 + 6 * p + 3 * a
-        pieces = [tiles(-1, at, 2), tiles(0, at, 0, 2), tiles(1, at, 0)]
+        pieces = [tiles(-1, at, 1), tiles(0, at, 0, 1), tiles(1, at, 0)]
     else:
-        at = 6 * p + 3 * a if level == 2 else 12 + 3 * a
-        pieces = [tiles(dy, at, 1) for dy in (-1, 0, 1)]
+        pieces = []
+        for dy in range(3):
+            key = (level, dz, dy, side)
+            if key not in seen:
+                seen[key] = off_row(strips[dz + 3, dy, side, level + 6 : level + 7], 16)
+            cells = seen[key]
+            pieces.append(pltpu.roll(cells, (first - 6 * p - 3 * a) % LANES, 1))
         if level == 3:
             pieces = [pieces[0], put(iota((8, LANES), 0) < 4, pieces[1], pieces[2])]
     return jnp.concatenate(pieces, axis=0)
 
 
-def own(fine, second, deep, level, a, z):
+def own(fine, second, deep, level, a, z, seen):
     if level == 0:
         return fine[a, z + 3]
     if level == 1:
         return pltpu.roll(second[z + 3], 64, 1) if a else second[z + 3]
     dz, p = z // DEPTH[level], z % DEPTH[level]
-    pieces = [deep[dz + 3, dy, p] for dy in range(3)]
-    if level == 3:
-        pieces = [pieces[0], put(iota((8, LANES), 0) < 4, pieces[1], pieces[2])]
-    cells = jnp.concatenate(pieces, axis=0)
-    first = 32 * a if level == 2 else 64 + 16 * a
-    return pltpu.roll(cells, (-first) % LANES, 1) if first else cells
+    if level == 2:
+        return pltpu.roll(jnp.concatenate([deep[dz + 3, dy, 0:8] for dy in range(3)], axis=0), (-64 * p - 32 * a) % LANES, 1)
+    if z not in seen:
+        seen[z] = [off_row(deep[dz + 3, dy, 8:9], 32) for dy in range(3)]
+    pieces = seen[z]
+    pieces = [pieces[0], put(iota((8, LANES), 0) < 4, pieces[1], pieces[2])]
+    return pltpu.roll(jnp.concatenate(pieces, axis=0), (-16 * a) % LANES, 1)
 
 
 def cycle(fine, second, deep, strips, corr_ref, res_ref, *spread):
     place = tuple(lax.axis_index(a) for a in AXES)
     count = tuple(lax.axis_size(a) for a in AXES)
-    solved, sources, centres = [], [], []
+    solved, sources, centres, seen = [], [], [], {}
     for level in range(4):
         d, rows, cols, tall = DEPTH[level], ROWS[level], COLS[level], TALL[level]
         lane, row = iota((tall, LANES), 1), iota((tall, LANES), 0)
@@ -230,8 +255,8 @@
             z_ok = (z_all >= 0) & (z_all < count[0] * d)
             both = []
             for a in range(2):
-                main = own(fine, second, deep, level, a, z)
-                sides = put(leftward, columns(strips, level, a, z, 0, LANES - HALO), columns(strips, level, a, z, 1, cols % LANES))
+                main = own(fine, second, deep, level, a, z, seen)
+                sides = put(leftward, columns(strips, level, a, z, 0, LANES - HALO, seen), columns(strips, level, a, z, 1, cols % LANES, seen))
                 both.append([main, sides] if level == 0 else [put(near, main, sides)])
             oks_z = [ok & z_ok for ok in oks]
             src.append([put(ok, v, 0.0) for ok, v in zip(oks_z, both[0])])
@@ -282,7 +307,7 @@
 def per_device(right_side, reaction):
     f32 = jnp.float32
     vmem = pl.BlockSpec(memory_space=pltpu.VMEM)
-    shapes = [(2, 14, 48, LANES), (10, 32, LANES), (7, 3, 2, 8, LANES), (7, 3, 2, 24, LANES)]
+    shapes = [(2, 14, 48, LANES), (10, 32, LANES), (7, 3, 16, LANES), (7, 3, 2, 24, LANES)]
     dma = pltpu.SemaphoreType.DMA
     blocks = 3 * len(NEAR) + len(FAR)
     extended = pl.pallas_call(

time: 37.1 us -> 32.2 us (0.87); the launches traced: 36.5 us -> 32 us
  Pallas kernels: 34.1 us -> 29.6 us
    pallas_call x1, Pallas kernels: 30.4 us -> 25.4 us  [per_device(): pl.pallas_call(exchange, out_shape=[jax.ShapeDtypeStruct(shape, f32) for...]
    pallas_call x1, Pallas kernels: 3.73 us -> 4.17 us  [per_device(): pl.pallas_call(cycle, out_shape=[block, block], in_specs=[vmem] * 4, out_...]
where the time goes in v3:
time: 32.2 us; the launch traced here: 32 us
  Pallas kernels  29.6 us (92%)
  local copies, waits for them, and re-layouts  1.8 us (6%)
  between operations  0.65 us (2%)
    pallas_call x1, Pallas kernels, per_device(): pl.pallas_call(exchange, out_shape=[jax.ShapeDtypeStruct(shape, f32) for...  25.4 us
    pallas_call x1, Pallas kernels, per_device(): pl.pallas_call(cycle, out_shape=[block, block], in_specs=[vmem] * 4, out_...  4.17 us
    unnamed x4, local copies, waits for them, and re-layouts  1.8 us

profile of v3, /device:TPU:1, one launch (start us, length us, event | category | flops | bytes accessed | tf_op | source)
XLA Modules:
  0.0 32.0 jit_solution(7852753180873280433)
XLA Ops:
  0.6 0.0 copy-start
  0.6 0.9 %copy-done = f32[8,32,128]{2,1,0:T(8,128)S(1)} copy-done((f32[8,32,128]{2,1,0:T(8,128)S(1)}, f32[8,32,128]{2,1,0:T(8,128)}, u32[]{:S(2)}) %copy-start) | copy-done | bytes 131096
  1.5 0.0 copy-start.1
  1.5 0.9 %copy-done.1 = f32[8,32,128]{2,1,0:T(8,128)S(1)} copy-done((f32[8,32,128]{2,1,0:T(8,128)S(1)}, f32[8,32,128]{2,1,0:T(8,128)}, u32[]{:S(2)}) %copy-start.1) | copy-done | bytes 131096
  2.4 25.4 %shard_map.41 = (f32[2,14,48,128]{3,2,1,0:T(8,128)S(1)}, f32[10,32,128]{2,1,0:T(8,128)S(1)}, f32[7,3,16,128]{3,2,1,0:T(8,128)S(1)}, f32[7,3,2,24,128]{4,3,2,1,0:T(8,128)S(1)}) custom-call(f32[8,32,128]{2,1,0:T(8,128)S(1)} %copy-done, f32[8,32,128]{2,1,0:T(8,128)S(1)} %copy-done.1), custom_call_target="tpu_custom_call" | custom-call | tf_op jit(solution)/shard_map/pallas_call | solution.py:313
  27.8 4.2 %shard_map.42 = (f32[8,32,128]{2,1,0:T(8,128)}, f32[8,32,128]{2,1,0:T(8,128)}) custom-call(f32[2,14,48,128]{3,2,1,0:T(8,128)S(1)} %get-tuple-element.6.fine, f32[10,32,128]{2,1,0:T(8,128)S(1)} %get-tuple-element.7.second, f32[7,3,16,128]{3,2,1,0:T(8,128)S(1)} %get-tuple-element.8.deep, f32[7,3,2,24,128]{4,3,2,1,0:T(8,128)S(1)} %get-tuple-element.9.strips), custom_call_target="tpu_custom_call" | custom-call | tf_op jit(solution)/shard_map/pallas_call | solution.py:339
Async XLA Ops:
  0.6 0.9 %copy-start = (f32[8,32,128]{2,1,0:T(8,128)S(1)}, f32[8,32,128]{2,1,0:T(8,128)}, u32[]{:S(2)}) copy-start(f32[8,32,128]{2,1,0:T(8,128)} %s_hbm.1) | copy-start | bytes 393220
  1.5 0.9 %copy-start.1 = (f32[8,32,128]{2,1,0:T(8,128)S(1)}, f32[8,32,128]{2,1,0:T(8,128)}, u32[]{:S(2)}) copy-start(f32[8,32,128]{2,1,0:T(8,128)} %c_hbm.1) | copy-start | bytes 393220

commit v4 on v3

--- a/solution.py
+++ b/solution.py
@@ -11,7 +11,6 @@
 MESH = pl.DeviceIdType.MESH
 AXES = ("grp", "gy", "gx")
 TAUS = tuple(1.0 / (1.15 + 0.85 * math.cos((2 * k - 1) * math.pi / 6.0)) for k in (1, 2, 3))
-EXACT = lax.Precision.HIGHEST
 LANES = 128
 HALO = 3
 DEPTH = (8, 4, 2, 1)
@@ -30,6 +29,17 @@
     return jnp.where(cond, value, other)
 
 
+def exact_dot(rows, pick):
+    high = rows.astype(jnp.bfloat16)
+    rest = rows - high.astype(jnp.float32)
+    middle = rest.astype(jnp.bfloat16)
+    low = (rest - middle.astype(jnp.float32)).astype(jnp.bfloat16)
+    terms = jnp.concatenate([high, middle, low], axis=0)
+    out = jnp.dot(terms, pick.astype(jnp.bfloat16), preferred_element_type=jnp.float32)
+    n = rows.shape[0]
+    return out[:n] + out[n : 2 * n] + out[2 * n :]
+
+
 def slide(cells, width):
     row = iota(cells.shape, 0)
     for k in (1, 2, 4):
@@ -45,7 +55,7 @@
     return slide(jnp.broadcast_to(row, (8, LANES)), LANES - width)
 
 
-def exchange(s_hbm, c_hbm, fine, second, deep, strips, sums2, sums3, sums4, msg, in_sem, xs, xr, bs, br, fs, fr):
+def exchange(both, fine, second, deep, strips, sums2, sums3, sums4, msg, xs, xr, bs, br, fs, fr):
     place = tuple(lax.axis_index(a) for a in AXES)
     count = tuple(lax.axis_size(a) for a in AXES)
 
@@ -69,13 +79,7 @@
         def _():
             pl.semaphore_signal(barrier, inc=1, device_id=device(*peer), device_id_type=MESH)
 
-    loads = []
-    for a, ref in enumerate((s_hbm, c_hbm)):
-        load = pltpu.make_async_copy(ref, fine.at[a, 3:11, 8:40, :], in_sem.at[a])
-        load.start()
-        loads.append(load)
-    for load in loads:
-        load.wait()
+    fine[:, 3:11, 8:40, :] = both[...]
 
     for a in range(2):
         for k in range(4):
@@ -86,14 +90,16 @@
         sums4[a, 0:4] = last
         sums4[a, 4:8] = jnp.zeros_like(last)
 
-    def mean(level, rows, first):
-        pick = jnp.where((iota((LANES, LANES), 0) >> level) + first == iota((LANES, LANES), 1), 0.125**level, 0.0)
-        return jnp.dot(rows, pick, precision=EXACT, preferred_element_type=jnp.float32)
-
-    level2 = sum(mean(1, sums2[a].reshape(64, LANES), 64 * a) for a in range(2))
-    second[3:7, 8:24, :] = level2.reshape(4, 16, LANES)
-    level3 = sum(mean(2, sums3[a, z], 64 * z + 32 * a) for a in range(2) for z in range(2))
-    level4 = in_row(sum(mean(3, sums4[a], 16 * a) for a in range(2)), 32)
+    def mean(level, rows):
+        pick = jnp.where((iota((LANES, LANES), 0) >> level) == iota((LANES, LANES), 1), 0.125**level, 0.0)
+        return exact_dot(rows, pick)
+
+    level2 = mean(1, sums2[...].reshape(128, LANES))
+    second[3:7, 8:24, :] = (level2[:64] + pltpu.roll(level2[64:], 64, 1)).reshape(4, 16, LANES)
+    level3 = mean(2, sums3[...].reshape(32, LANES))
+    level3 = sum(pltpu.roll(level3[16 * a + 8 * z : 16 * a + 8 * z + 8], 64 * z + 32 * a, 1) for a in range(2) for z in range(2))
+    level4 = mean(3, sums4[...].reshape(16, LANES))
+    level4 = in_row(level4[:8] + pltpu.roll(level4[8:], 16, 1), 32)
     deep[3, 1, 0:8] = level3
     deep[3, 1, 8:9] = level4
 
@@ -285,9 +291,9 @@
         coarse = DEPTH[level + 1]
         for n in range(coarse + 2):
             buf[n] = total[n + 2][0]
+        halves = exact_dot(jnp.concatenate([buf[n, 4 : 4 + tall // 2, :] for n in range(coarse + 2)], axis=0), pick)
         for n in range(coarse + 2):
-            half = buf[n, 4 : 4 + tall // 2, :]
-            half = jnp.dot(half, pick, precision=EXACT, preferred_element_type=jnp.float32)
+            half = halves[n * (tall // 2) : (n + 1) * (tall // 2)]
             for dy in range(2):
                 for k in range(width // LANES):
                     wide[n, k, pl.ds(dy, tall // 2, stride=2), :] = half[:, k * LANES : (k + 1) * LANES]
@@ -313,7 +319,7 @@
     extended = pl.pallas_call(
         exchange,
         out_shape=[jax.ShapeDtypeStruct(shape, f32) for shape in shapes],
-        in_specs=[pl.BlockSpec(memory_space=pltpu.HBM)] * 2,
+        in_specs=[vmem],
         out_specs=[vmem] * 4,
         scratch_shapes=[
             pltpu.VMEM((2, 4, 16, LANES), f32),
@@ -322,14 +328,13 @@
             pltpu.VMEM((2, 24, LANES), f32),
             dma((2,)),
             dma((2,)),
-            dma((2,)),
             dma((blocks,)),
             dma((blocks,)),
             dma((20,)),
             dma((20,)),
         ],
         compiler_params=pltpu.CompilerParams(collective_id=0, has_side_effects=True, vmem_limit_bytes=16 * 1024 * 1024),
-    )(right_side, reaction)
+    )(jnp.stack([right_side, reaction]))
     block = jax.ShapeDtypeStruct(right_side.shape, f32)
     spread = []
     for level in (0, 1, 2):

time: 32.2 us -> 30.9 us (0.960)
  local copies, waits for them, and re-layouts: 1.8 us -> 0 us
  other arithmetic: 0 us -> 0.99 us
  Pallas kernels: 29.6 us -> 29.1 us
    unnamed x4 -> x0, local copies, waits for them, and re-layouts: 1.8 us -> none
    another operation x0 -> x1, other arithmetic: none -> 0.99 us  [per_device(): jnp.stack([right_side, reaction])]
    pallas_call x1, Pallas kernels: 4.17 us -> 3.72 us  [per_device(): pl.pallas_call(cycle, out_shape=[block, block], in_specs=[vmem] * 4, out_...]
where the time goes in v4:
time: 30.9 us; the launch traced here: 30.7 us
  Pallas kernels  29.1 us (94%)
  other arithmetic  0.99 us (3%)
  between operations  0.64 us (2%)
    pallas_call x1, Pallas kernels, per_device(): pl.pallas_call(exchange, out_shape=[jax.ShapeDtypeStruct(shape, f32) for...  25.4 us
    pallas_call x1, Pallas kernels, per_device(): pl.pallas_call(cycle, out_shape=[block, block], in_specs=[vmem] * 4, out_...  3.72 us
    another operation x1, other arithmetic, per_device(): jnp.stack([right_side, reaction])  0.99 us

profile of v4, /device:TPU:1, one launch (start us, length us, event | category | flops | bytes accessed | tf_op | source)
XLA Modules:
  0.0 30.7 jit_solution(12543353189056230585)
XLA Ops:
  0.6 1.0 %pad_maximum_fusion.both = f32[2,8,32,128]{3,2,1,0:T(8,128)S(1)} fusion(f32[1,8,32,128]{3,2,1,0:T(8,128)} %bitcast.2, f32[1,8,32,128]{3,2,1,0:T(8,128)} %bitcast.3), kind=kLoop, calls=%fused_computation | loop fusion | flops 65536 | bytes 524288 | tf_op jit(solution)/shard_map/stack | solution.py:337
  1.6 25.4 %shard_map.41 = (f32[2,14,48,128]{3,2,1,0:T(8,128)S(1)}, f32[10,32,128]{2,1,0:T(8,128)S(1)}, f32[7,3,16,128]{3,2,1,0:T(8,128)S(1)}, f32[7,3,2,24,128]{4,3,2,1,0:T(8,128)S(1)}) custom-call(f32[2,8,32,128]{3,2,1,0:T(8,128)S(1)} %pad_maximum_fusion.both), custom_call_target="tpu_custom_call" | custom-call | tf_op jit(solution)/shard_map/pallas_call | solution.py:319
  27.0 3.7 %shard_map.42 = (f32[8,32,128]{2,1,0:T(8,128)}, f32[8,32,128]{2,1,0:T(8,128)}) custom-call(f32[2,14,48,128]{3,2,1,0:T(8,128)S(1)} %get-tuple-element.6.fine, f32[10,32,128]{2,1,0:T(8,128)S(1)} %get-tuple-element.7.second, f32[7,3,16,128]{3,2,1,0:T(8,128)S(1)} %get-tuple-element.8.deep, f32[7,3,2,24,128]{4,3,2,1,0:T(8,128)S(1)} %get-tuple-element.9.strips), custom_call_target="tpu_custom_call" | custom-call | tf_op jit(solution)/shard_map/pallas_call | solution.py:344

commit v5 on v4

--- a/solution.py
+++ b/solution.py
@@ -140,43 +140,60 @@
     pl.semaphore_wait(barrier, expected)
 
     def remote(src, dst, sems, n, *peer):
-        copy = pltpu.make_async_remote_copy(
+        return pltpu.make_async_remote_copy(
             src_ref=src, dst_ref=dst, send_sem=sems[0].at[n], recv_sem=sems[1].at[n], device_id=device(*peer), device_id_type=MESH
         )
-        pl.when(exists(*peer))(copy.start)
-        return copy, exists(*peer), exists(*(-step for step in peer))
-
-    def landed(copies):
-        for copy, _, fro in copies:
-            pl.when(fro)(copy.wait_recv)
-
-    across = [remote(msg.at[side, 0:18], strips.at[3, 1, 1 - side, 0:18], (xs, xr), side, 0, 0, 2 * side - 1) for side in range(2)]
-
-    blocks = []
-    for dz, dy in NEAR + FAR:
+
+    def each(copies, do, *peer):
+        @pl.when(exists(*peer))
+        def _():
+            for copy in copies:
+                getattr(copy, do)()
+
+    across = {}
+    for side, dx in enumerate((-1, 1)):
+        across[dx] = [remote(msg.at[side, 0:18], strips.at[3, 1, 1 - side, 0:18], (xs, xr), side, 0, 0, dx)]
+        each(across[dx], "start", 0, 0, dx)
+
+    blocks, n = {}, 0
+    for dz, dy in NEAR:
+        refs = [(deep.at[3, 1, 0:9], deep.at[3 - dz, 1 - dy, 0:9])]
         for ref, depth, rows in ((fine, 8, 32), (second, 4, 16)):
-            if abs(dz) > 1:
-                continue
             z0, z1 = {-1: (3, 6), 0: (3, 3 + depth), 1: (depth, 3 + depth)}[dz]
             y0, y1 = {-1: (8, 11), 0: (8, 8 + rows), 1: (rows + 5, rows + 8)}[dy]
             up, along = z0 - dz * depth, y0 - dy * rows
-            src, dst = ref, ref
             if ref is fine:
-                src, dst = fine.at[:, z0:z1, y0:y1, :], fine.at[:, up : up + z1 - z0, along : along + y1 - y0, :]
+                refs.append((fine.at[:, z0:z1, y0:y1, :], fine.at[:, up : up + z1 - z0, along : along + y1 - y0, :]))
             else:
-                src, dst = second.at[z0:z1, y0:y1, :], second.at[up : up + z1 - z0, along : along + y1 - y0, :]
-            blocks.append(remote(src, dst, (bs, br), len(blocks), dz, dy, 0))
-        rows = slice(8, 9) if abs(dz) == 3 else slice(0, 9)
-        blocks.append(remote(deep.at[3, 1, rows], deep.at[3 - dz, 1 - dy, rows], (bs, br), len(blocks), dz, dy, 0))
-
-    landed(across)
-    passed = []
+                refs.append((second.at[z0:z1, y0:y1, :], second.at[up : up + z1 - z0, along : along + y1 - y0, :]))
+        blocks[dz, dy] = [remote(src, dst, (bs, br), n + k, dz, dy, 0) for k, (src, dst) in enumerate(refs)]
+        n += len(refs)
+        each(blocks[dz, dy], "start", dz, dy, 0)
+
+    for dx in (-1, 1):
+        each(across[dx], "wait_recv", 0, 0, -dx)
+    for side in range(2):
+        deep[3, 1, 9 + 2 * side : 11 + 2 * side] = strips[3, 1, side, 8:10]
+    passed = {}
     for dz, dy in FAR + NEAR:
-        rows = slice(8, 10) if abs(dz) > 1 else {-1: slice(8, 13), 0: slice(0, 18), 1: slice(5, 10)}[dy]
-        passed.append(remote(strips.at[3, 1, :, rows, :], strips.at[3 - dz, 1 - dy, :, rows, :], (fs, fr), len(passed), dz, dy, 0))
-    landed(blocks + passed)
-    for copy, to, _ in across + blocks + passed:
-        pl.when(to)(copy.wait_send)
+        if abs(dz) > 1:
+            rows = slice(8, 13) if abs(dz) == 3 else slice(0, 13)
+            src, dst = deep.at[3, 1, rows], deep.at[3 - dz, 1 - dy, rows]
+        else:
+            rows = {-1: slice(8, 13), 0: slice(0, 18), 1: slice(5, 10)}[dy]
+            src, dst = strips.at[3, 1, :, rows, :], strips.at[3 - dz, 1 - dy, :, rows, :]
+        passed[dz, dy] = [remote(src, dst, (fs, fr), len(passed), dz, dy, 0)]
+        each(passed[dz, dy], "start", dz, dy, 0)
+    for dx in (-1, 1):
+        each(across[dx], "wait_send", 0, 0, dx)
+    for dz, dy in NEAR:
+        each(blocks[dz, dy], "wait_send", dz, dy, 0)
+    for dz, dy in NEAR:
+        each(blocks[dz, dy] + passed[dz, dy], "wait_recv", -dz, -dy, 0)
+    for dz, dy in FAR:
+        each(passed[dz, dy], "wait_recv", -dz, -dy, 0)
+    for dz, dy in NEAR + FAR:
+        each(passed[dz, dy], "wait_send", dz, dy, 0)
 
 
 def ring_roll(chunks, shift):
@@ -198,7 +215,7 @@
     return [b + 2.0 * v + f for b, v, f in zip(before, out, after)]
 
 
-def columns(strips, level, a, z, side, first, seen):
+def columns(deep, strips, level, a, z, side, first, seen):
     dz, p = z // DEPTH[level], z % DEPTH[level]
 
     def tiles(dy, lane, *which):
@@ -217,7 +234,9 @@
         for dy in range(3):
             key = (level, dz, dy, side)
             if key not in seen:
-                seen[key] = off_row(strips[dz + 3, dy, side, level + 6 : level + 7], 16)
+                near, far = level + 6, 7 + 2 * side + level
+                row = strips[dz + 3, dy, side, near : near + 1] if abs(dz) < 2 else deep[dz + 3, dy, far : far + 1]
+                seen[key] = off_row(row, 16)
             cells = seen[key]
             pieces.append(pltpu.roll(cells, (first - 6 * p - 3 * a) % LANES, 1))
         if level == 3:
@@ -262,7 +281,7 @@
             both = []
             for a in range(2):
                 main = own(fine, second, deep, level, a, z, seen)
-                sides = put(leftward, columns(strips, level, a, z, 0, LANES - HALO, seen), columns(strips, level, a, z, 1, cols % LANES, seen))
+                sides = put(leftward, columns(deep, strips, level, a, z, 0, LANES - HALO, seen), columns(deep, strips, level, a, z, 1, cols % LANES, seen))
                 both.append([main, sides] if level == 0 else [put(near, main, sides)])
             oks_z = [ok & z_ok for ok in oks]
             src.append([put(ok, v, 0.0) for ok, v in zip(oks_z, both[0])])
@@ -315,7 +334,7 @@
     vmem = pl.BlockSpec(memory_space=pltpu.VMEM)
     shapes = [(2, 14, 48, LANES), (10, 32, LANES), (7, 3, 16, LANES), (7, 3, 2, 24, LANES)]
     dma = pltpu.SemaphoreType.DMA
-    blocks = 3 * len(NEAR) + len(FAR)
+    blocks = 3 * len(NEAR)
     extended = pl.pallas_call(
         exchange,
         out_shape=[jax.ShapeDtypeStruct(shape, f32) for shape in shapes],

time: 30.9 us -> 30.1 us (0.974)
  Pallas kernels: 29.1 us -> 28.2 us
    pallas_call x1, Pallas kernels: 25.4 us -> 24.5 us  [per_device(): pl.pallas_call(exchange, out_shape=[jax.ShapeDtypeStruct(shape, f32) for...]
where the time goes in v5:
time: 30.1 us; the launch traced here: 29.8 us
  Pallas kernels  28.2 us (94%)
  other arithmetic  0.99 us (3%)
  between operations  0.64 us (2%)
    pallas_call x1, Pallas kernels, per_device(): pl.pallas_call(exchange, out_shape=[jax.ShapeDtypeStruct(shape, f32) for...  24.5 us
    pallas_call x1, Pallas kernels, per_device(): pl.pallas_call(cycle, out_shape=[block, block], in_specs=[vmem] * 4, out_...  3.72 us
    another operation x1, other arithmetic, per_device(): jnp.stack([right_side, reaction])  0.99 us

profile of v5, /device:TPU:1, one launch (start us, length us, event | category | flops | bytes accessed | tf_op | source)
XLA Modules:
  0.0 29.8 jit_solution(4796935810417418230)
XLA Ops:
  0.6 1.0 %pad_maximum_fusion.both = f32[2,8,32,128]{3,2,1,0:T(8,128)S(1)} fusion(f32[1,8,32,128]{3,2,1,0:T(8,128)} %bitcast.2, f32[1,8,32,128]{3,2,1,0:T(8,128)} %bitcast.3), kind=kLoop, calls=%fused_computation | loop fusion | flops 65536 | bytes 524288 | tf_op jit(solution)/shard_map/stack | solution.py:356
  1.6 24.5 %shard_map.41 = (f32[2,14,48,128]{3,2,1,0:T(8,128)S(1)}, f32[10,32,128]{2,1,0:T(8,128)S(1)}, f32[7,3,16,128]{3,2,1,0:T(8,128)S(1)}, f32[7,3,2,24,128]{4,3,2,1,0:T(8,128)S(1)}) custom-call(f32[2,8,32,128]{3,2,1,0:T(8,128)S(1)} %pad_maximum_fusion.both), custom_call_target="tpu_custom_call" | custom-call | tf_op jit(solution)/shard_map/pallas_call | solution.py:338
  26.1 3.7 %shard_map.42 = (f32[8,32,128]{2,1,0:T(8,128)}, f32[8,32,128]{2,1,0:T(8,128)}) custom-call(f32[2,14,48,128]{3,2,1,0:T(8,128)S(1)} %get-tuple-element.6.fine, f32[10,32,128]{2,1,0:T(8,128)S(1)} %get-tuple-element.7.second, f32[7,3,16,128]{3,2,1,0:T(8,128)S(1)} %get-tuple-element.8.deep, f32[7,3,2,24,128]{4,3,2,1,0:T(8,128)S(1)} %get-tuple-element.9.strips), custom_call_target="tpu_custom_call" | custom-call | tf_op jit(solution)/shard_map/pallas_call | solution.py:363

commit v6 on v5

--- a/solution.py
+++ b/solution.py
@@ -18,7 +18,7 @@
 COLS = (128, 64, 32, 16)
 TALL = (48, 32, 24, 16)
 NEAR = tuple((dz, dy) for dz in (-1, 0, 1) for dy in (-1, 0, 1) if dz or dy)
-FAR = tuple((dz, dy) for dz in (-3, 3, -2, 2) for dy in (-1, 0, 1))
+FAR = (-3, 3, -2, 2)
 
 
 def iota(shape, dim):
@@ -71,7 +71,7 @@
     def device(*steps):
         return tuple(p + step for p, step in zip(place, steps))
 
-    peers = [(0, 0, -1), (0, 0, 1)] + [(dz, dy, 0) for dz, dy in FAR + NEAR]
+    peers = [(dz, 0, dx) for dz in (0, *FAR) for dx in (-1, 1)] + [(dz, 0, 0) for dz in FAR] + [(dz, dy, 0) for dz, dy in NEAR]
     barrier = pltpu.get_barrier_semaphore()
     for peer in peers:
 
@@ -154,10 +154,22 @@
     for side, dx in enumerate((-1, 1)):
         across[dx] = [remote(msg.at[side, 0:18], strips.at[3, 1, 1 - side, 0:18], (xs, xr), side, 0, 0, dx)]
         each(across[dx], "start", 0, 0, dx)
-
-    blocks, n = {}, 0
+    distant, m = {}, 2
+    for dz in FAR:
+        for side, dx in enumerate((-1, 1)):
+            at = 9 + 2 * (1 - side)
+            distant[dz, dx] = [remote(msg.at[side, 8:10], deep.at[3 - dz, 1, at : at + 2], (xs, xr), m, dz, 0, dx)]
+            each(distant[dz, dx], "start", dz, 0, dx)
+            m += 1
+
+    column = {}
+    for dz in (-1, 1, *FAR):
+        rows = slice(8, 9) if abs(dz) == 3 else slice(0, 9)
+        column[dz] = [remote(deep.at[3, 1, rows], deep.at[3 - dz, 1, rows], (bs, br), len(column), dz, 0, 0)]
+        each(column[dz], "start", dz, 0, 0)
+    blocks, n = {}, len(column)
     for dz, dy in NEAR:
-        refs = [(deep.at[3, 1, 0:9], deep.at[3 - dz, 1 - dy, 0:9])]
+        refs = []
         for ref, depth, rows in ((fine, 8, 32), (second, 4, 16)):
             z0, z1 = {-1: (3, 6), 0: (3, 3 + depth), 1: (depth, 3 + depth)}[dz]
             y0, y1 = {-1: (8, 11), 0: (8, 8 + rows), 1: (rows + 5, rows + 8)}[dy]
@@ -172,28 +184,37 @@
 
     for dx in (-1, 1):
         each(across[dx], "wait_recv", 0, 0, -dx)
-    for side in range(2):
-        deep[3, 1, 9 + 2 * side : 11 + 2 * side] = strips[3, 1, side, 8:10]
     passed = {}
-    for dz, dy in FAR + NEAR:
-        if abs(dz) > 1:
-            rows = slice(8, 13) if abs(dz) == 3 else slice(0, 13)
-            src, dst = deep.at[3, 1, rows], deep.at[3 - dz, 1 - dy, rows]
-        else:
-            rows = {-1: slice(8, 13), 0: slice(0, 18), 1: slice(5, 10)}[dy]
-            src, dst = strips.at[3, 1, :, rows, :], strips.at[3 - dz, 1 - dy, :, rows, :]
+    for dz, dy in NEAR:
+        rows = {-1: slice(8, 13), 0: slice(0, 18), 1: slice(5, 10)}[dy]
+        src, dst = strips.at[3, 1, :, rows, :], strips.at[3 - dz, 1 - dy, :, rows, :]
         passed[dz, dy] = [remote(src, dst, (fs, fr), len(passed), dz, dy, 0)]
         each(passed[dz, dy], "start", dz, dy, 0)
+    for dz in (-1, 1, *FAR):
+        each(column[dz], "wait_recv", -dz, 0, 0)
+    for dz, dx in distant:
+        each(distant[dz, dx], "wait_recv", -dz, 0, -dx)
+    along = {}
+    for dy in (-1, 1):
+        src, dst = deep.at[:, 1, 0:13, :], deep.at[:, 1 - dy, 0:13, :]
+        along[dy] = [remote(src, dst, (fs, fr), len(passed) + len(along), 0, dy, 0)]
+        each(along[dy], "start", 0, dy, 0)
     for dx in (-1, 1):
         each(across[dx], "wait_send", 0, 0, dx)
+    for dz, dx in distant:
+        each(distant[dz, dx], "wait_send", dz, 0, dx)
+    for dz in (-1, 1, *FAR):
+        each(column[dz], "wait_send", dz, 0, 0)
     for dz, dy in NEAR:
         each(blocks[dz, dy], "wait_send", dz, dy, 0)
     for dz, dy in NEAR:
         each(blocks[dz, dy] + passed[dz, dy], "wait_recv", -dz, -dy, 0)
-    for dz, dy in FAR:
-        each(passed[dz, dy], "wait_recv", -dz, -dy, 0)
-    for dz, dy in NEAR + FAR:
+    for dy in (-1, 1):
+        each(along[dy], "wait_recv", 0, -dy, 0)
+    for dz, dy in NEAR:
         each(passed[dz, dy], "wait_send", dz, dy, 0)
+    for dy in (-1, 1):
+        each(along[dy], "wait_send", 0, dy, 0)
 
 
 def ring_roll(chunks, shift):
@@ -334,7 +355,7 @@
     vmem = pl.BlockSpec(memory_space=pltpu.VMEM)
     shapes = [(2, 14, 48, LANES), (10, 32, LANES), (7, 3, 16, LANES), (7, 3, 2, 24, LANES)]
     dma = pltpu.SemaphoreType.DMA
-    blocks = 3 * len(NEAR)
+    blocks = 2 * len(NEAR) + 6
     extended = pl.pallas_call(
         exchange,
         out_shape=[jax.ShapeDtypeStruct(shape, f32) for shape in shapes],
@@ -345,12 +366,12 @@
             pltpu.VMEM((2, 2, 8, LANES), f32),
             pltpu.VMEM((2, 8, LANES), f32),
             pltpu.VMEM((2, 24, LANES), f32),
-            dma((2,)),
-            dma((2,)),
+            dma((10,)),
+            dma((10,)),
             dma((blocks,)),
             dma((blocks,)),
-            dma((20,)),
-            dma((20,)),
+            dma((10,)),
+            dma((10,)),
         ],
         compiler_params=pltpu.CompilerParams(collective_id=0, has_side_effects=True, vmem_limit_bytes=16 * 1024 * 1024),
     )(jnp.stack([right_side, reaction]))

time: 30.1 us -> 29.4 us (0.977)
  Pallas kernels: 28.2 us -> 27.6 us
    pallas_call x1, Pallas kernels: 24.5 us -> 23.9 us  [per_device(): pl.pallas_call(exchange, out_shape=[jax.ShapeDtypeStruct(shape, f32) for...]
where the time goes in v6:
time: 29.4 us; the launch traced here: 29.3 us
  Pallas kernels  27.6 us (94%)
  other arithmetic  0.99 us (3%)
  between operations  0.64 us (2%)
    pallas_call x1, Pallas kernels, per_device(): pl.pallas_call(exchange, out_shape=[jax.ShapeDtypeStruct(shape, f32) for...  23.9 us
    pallas_call x1, Pallas kernels, per_device(): pl.pallas_call(cycle, out_shape=[block, block], in_specs=[vmem] * 4, out_...  3.72 us
    another operation x1, other arithmetic, per_device(): jnp.stack([right_side, reaction])  0.99 us

profile of v6, /device:TPU:1, one launch (start us, length us, event | category | flops | bytes accessed | tf_op | source)
XLA Modules:
  0.0 29.3 jit_solution(1245341912045562459)
XLA Ops:
  0.6 1.0 %pad_maximum_fusion.both = f32[2,8,32,128]{3,2,1,0:T(8,128)S(1)} fusion(f32[1,8,32,128]{3,2,1,0:T(8,128)} %bitcast.2, f32[1,8,32,128]{3,2,1,0:T(8,128)} %bitcast.3), kind=kLoop, calls=%fused_computation | loop fusion | flops 65536 | bytes 524288 | tf_op jit(solution)/shard_map/stack | solution.py:377
  1.6 23.9 %shard_map.41 = (f32[2,14,48,128]{3,2,1,0:T(8,128)S(1)}, f32[10,32,128]{2,1,0:T(8,128)S(1)}, f32[7,3,16,128]{3,2,1,0:T(8,128)S(1)}, f32[7,3,2,24,128]{4,3,2,1,0:T(8,128)S(1)}) custom-call(f32[2,8,32,128]{3,2,1,0:T(8,128)S(1)} %pad_maximum_fusion.both), custom_call_target="tpu_custom_call" | custom-call | tf_op jit(solution)/shard_map/pallas_call | solution.py:359
  25.5 3.7 %shard_map.42 = (f32[8,32,128]{2,1,0:T(8,128)}, f32[8,32,128]{2,1,0:T(8,128)}) custom-call(f32[2,14,48,128]{3,2,1,0:T(8,128)S(1)} %get-tuple-element.6.fine, f32[10,32,128]{2,1,0:T(8,128)S(1)} %get-tuple-element.7.second, f32[7,3,16,128]{3,2,1,0:T(8,128)S(1)} %get-tuple-element.8.deep, f32[7,3,2,24,128]{4,3,2,1,0:T(8,128)S(1)} %get-tuple-element.9.strips), custom_call_target="tpu_custom_call" | custom-call | tf_op jit(solution)/shard_map/pallas_call | solution.py:384

commit v7 on v6

--- a/solution.py
+++ b/solution.py
@@ -17,7 +17,7 @@
 ROWS = (32, 16, 8, 4)
 COLS = (128, 64, 32, 16)
 TALL = (48, 32, 24, 16)
-NEAR = tuple((dz, dy) for dz in (-1, 0, 1) for dy in (-1, 0, 1) if dz or dy)
+NEAR = ((0, -1), (0, 1), (-1, -1), (-1, 1), (1, -1), (1, 1), (-1, 0), (1, 0))
 FAR = (-3, 3, -2, 2)
 
 
@@ -71,7 +71,7 @@
     def device(*steps):
         return tuple(p + step for p, step in zip(place, steps))
 
-    peers = [(dz, 0, dx) for dz in (0, *FAR) for dx in (-1, 1)] + [(dz, 0, 0) for dz in FAR] + [(dz, dy, 0) for dz, dy in NEAR]
+    peers = [(dz, 0, 0) for dz in FAR] + [(0, 0, -1), (0, 0, 1)] + [(dz, dy, 0) for dz, dy in NEAR] + [(dz, 0, dx) for dz in FAR for dx in (-1, 1)]
     barrier = pltpu.get_barrier_semaphore()
     for peer in peers:
 
@@ -154,6 +154,11 @@
     for side, dx in enumerate((-1, 1)):
         across[dx] = [remote(msg.at[side, 0:18], strips.at[3, 1, 1 - side, 0:18], (xs, xr), side, 0, 0, dx)]
         each(across[dx], "start", 0, 0, dx)
+    column = {}
+    for dz in (-1, 1, *FAR):
+        rows = slice(8, 9) if abs(dz) == 3 else slice(0, 9)
+        column[dz] = [remote(deep.at[3, 1, rows], deep.at[3 - dz, 1, rows], (bs, br), len(column), dz, 0, 0)]
+        each(column[dz], "start", dz, 0, 0)
     distant, m = {}, 2
     for dz in FAR:
         for side, dx in enumerate((-1, 1)):
@@ -161,12 +166,6 @@
             distant[dz, dx] = [remote(msg.at[side, 8:10], deep.at[3 - dz, 1, at : at + 2], (xs, xr), m, dz, 0, dx)]
             each(distant[dz, dx], "start", dz, 0, dx)
             m += 1
-
-    column = {}
-    for dz in (-1, 1, *FAR):
-        rows = slice(8, 9) if abs(dz) == 3 else slice(0, 9)
-        column[dz] = [remote(deep.at[3, 1, rows], deep.at[3 - dz, 1, rows], (bs, br), len(column), dz, 0, 0)]
-        each(column[dz], "start", dz, 0, 0)
     blocks, n = {}, len(column)
     for dz, dy in NEAR:
         refs = []

time: 29.4 us -> 29.4 us (level)
  no operation moved by 1% of the time
where the time goes in v7:
time: 29.4 us; the launch traced here: 29.3 us
  Pallas kernels  27.6 us (94%)
  other arithmetic  0.99 us (3%)
  between operations  0.64 us (2%)
    pallas_call x1, Pallas kernels, per_device(): pl.pallas_call(exchange, out_shape=[jax.ShapeDtypeStruct(shape, f32) for...  23.9 us
    pallas_call x1, Pallas kernels, per_device(): pl.pallas_call(cycle, out_shape=[block, block], in_specs=[vmem] * 4, out_...  3.72 us
    another operation x1, other arithmetic, per_device(): jnp.stack([right_side, reaction])  0.99 us

profile of v7, /device:TPU:1, one launch (start us, length us, event | category | flops | bytes accessed | tf_op | source)
XLA Modules:
  0.0 29.3 jit_solution(5047212412667168128)
XLA Ops:
  0.6 1.0 %pad_maximum_fusion.both = f32[2,8,32,128]{3,2,1,0:T(8,128)S(1)} fusion(f32[1,8,32,128]{3,2,1,0:T(8,128)} %bitcast.2, f32[1,8,32,128]{3,2,1,0:T(8,128)} %bitcast.3), kind=kLoop, calls=%fused_computation | loop fusion | flops 65536 | bytes 524288 | tf_op jit(solution)/shard_map/stack | solution.py:376
  1.6 23.9 %shard_map.41 = (f32[2,14,48,128]{3,2,1,0:T(8,128)S(1)}, f32[10,32,128]{2,1,0:T(8,128)S(1)}, f32[7,3,16,128]{3,2,1,0:T(8,128)S(1)}, f32[7,3,2,24,128]{4,3,2,1,0:T(8,128)S(1)}) custom-call(f32[2,8,32,128]{3,2,1,0:T(8,128)S(1)} %pad_maximum_fusion.both), custom_call_target="tpu_custom_call" | custom-call | tf_op jit(solution)/shard_map/pallas_call | solution.py:358
  25.5 3.7 %shard_map.42 = (f32[8,32,128]{2,1,0:T(8,128)}, f32[8,32,128]{2,1,0:T(8,128)}) custom-call(f32[2,14,48,128]{3,2,1,0:T(8,128)S(1)} %get-tuple-element.6.fine, f32[10,32,128]{2,1,0:T(8,128)S(1)} %get-tuple-element.7.second, f32[7,3,16,128]{3,2,1,0:T(8,128)S(1)} %get-tuple-element.8.deep, f32[7,3,2,24,128]{4,3,2,1,0:T(8,128)S(1)} %get-tuple-element.9.strips), custom_call_target="tpu_custom_call" | custom-call | tf_op jit(solution)/shard_map/pallas_call | solution.py:383
